TPU v7x, 32 devices: a whole 2x2x4 slice. The times are simulated.
32 devices in a mesh: dp: 8 (over z, core), seq: 4 (over y, x).
Axes of the slice: x: 2, y: 2, z: 4, core: 2. Of those that a mesh axis runs over, the one named last changes fastest.
Arguments:
- inputs: bfloat16 [16, 1024, 512], P('dp', 'seq'), may hold values from -3 to 3
- segment_ids: int32 [16, 1024], P('dp', 'seq'), may hold values from 0 to 3, never falling along the last dimension, each value on 1 to 800 neighbouring positions
- cotangent: bfloat16 [16, 1024, 512], P('dp', 'seq'), may hold values from -6 to 6
- norm_gain: bfloat16 [4, 512], P(None, 'seq'), may hold values from 0.5 to 1.5
- norm_bias: bfloat16 [4, 512], P(None, 'seq'), may hold values from -1.5 to 1.5
- glu_weight: bfloat16 [512, 1024], P('seq'), may hold values from -0.25 to 0.25
- left_weight: bfloat16 [512, 2048], P('seq'), may hold values from -0.25 to 0.25
- conv_weight: bfloat16 [3, 512, 256], P(None, 'seq'), may hold values from -0.75 to 0.75
- mid_gain: bfloat16 [2048], P('seq'), may hold values from 0.5 to 1.5
- mid_bias: bfloat16 [2048], P('seq'), may hold values from -1.5 to 1.5
- depth_weight: bfloat16 [9, 2048], P(None, 'seq'), may hold values from -2 to 2
- point_weight: bfloat16 [2048, 512], P('seq'), may hold values from -0.125 to 0.125
- qkv_weight: bfloat16 [512, 1536], P('seq'), may hold values from -0.25 to 0.25
- out_weight: bfloat16 [512, 512], P('seq'), may hold values from -1 to 1
- ffn_in: bfloat16 [512, 2048], P('seq'), may hold values from -0.25 to 0.25
- ffn_out: bfloat16 [2048, 512], P('seq'), may hold values from -0.1875 to 0.1875
Outputs:
- output: float32 [16, 1024, 512], P('dp', 'seq')
- input_grad: float32 [16, 1024, 512], P('dp', 'seq')
- grad_norm_gain: float32 [4, 512], P(None, 'seq')
- grad_norm_bias: float32 [4, 512], P(None, 'seq')
- grad_glu_weight: float32 [512, 1024], P('seq')
- grad_left_weight: float32 [512, 2048], P('seq')
- grad_conv_weight: float32 [3, 512, 256], P(None, 'seq')
- grad_mid_gain: float32 [2048], P('seq')
- grad_mid_bias: float32 [2048], P('seq')
- grad_depth_weight: float32 [9, 2048], P(None, 'seq')
- grad_point_weight: float32 [2048, 512], P('seq')
- grad_qkv_weight: float32 [512, 1536], P('seq')
- grad_out_weight: float32 [512, 512], P('seq')
- grad_ffn_in: float32 [512, 2048], P('seq')
- grad_ffn_out: float32 [2048, 512], P('seq')
Inputs may be any that keep to these rules, and one draw needn't show every extreme that they name: `segment_ids`: along each sequence of 1024 tokens the segment ids never fall and take every value from 0 to 3; each document has 1 to 800 tokens, and one document of every sequence has exactly 800.
All inputs are finite; a program needn't handle non-finite values.
Results may differ from a plain program's by a relative error of at most 0.02.
Values may be sent and summed in bfloat16 or wider, within the bound.
A program may use at most 192 MiB of HBM per device.

v0:
```python
import math

import jax
import jax.numpy as jnp
from jax import lax
from jax.experimental import pallas as pl
from jax.experimental.pallas import tpu as pltpu
from jax.sharding import PartitionSpec as P

HEADS = 8
EPS = 1e-06
MESH = pl.DeviceIdType.MESH
F32 = jnp.float32
BF16 = jnp.bfloat16

GLU, CONV, LEFT, POINT, QKV, OUT, FIN, FOUT = range(8)
WEIGHTS = 8
(U_GLU0, U_GLU1, U_CONV, U_LEFT0, U_LEFT1, U_POINT0, U_POINT1, U_QKV0, U_QKV1, U_OUT, U_FIN, U_FOUT, SMALL) = range(13)
UNITS = 13
UNIT_WEIGHT = (GLU, GLU, CONV, LEFT, LEFT, POINT, POINT, QKV, QKV, OUT, FIN, FOUT, WEIGHTS)
UNIT_PART = (0, 1, None, 0, 1, 0, 1, 0, 1, None, None, None, None)

SHARED = (GLU, LEFT, POINT, FIN,)
SMALLS, TOKENS = 8, 9
START = (GLU, SMALLS, LEFT, TOKENS)
FORWARD = (
    ((1, GLU),),
    (),
    (),
    ((1, LEFT), (2, GLU), (0, CONV), (2, LEFT), (0, POINT), (1, CONV), (0, QKV), (3, GLU)),
    (),
    ((1, POINT),),
    (),
    ((2, CONV), (3, LEFT), (0, OUT)),
    ((1, QKV),),
    (),
    (),
    (),
    ((0, FIN),),
    ((1, OUT), (2, POINT)),
    (),
    ((0, FOUT),),
    ((2, QKV),),
    ((1, FIN),),
    (),
    (),
    ((2, OUT),),
    (),
    ((3, POINT),),
    ((0, TOKENS),),
    (),
    (),
    ((1, FOUT),),
    (),
    ((2, FIN),),
    (),
    (),
    (),
    ((2, FOUT), (3, FIN)),
    (),
    (),
    (),
    (),
    (),
    (),
    (),
    (),
)
SCHEDULE = (
    (),
    (),
    (),
    (U_FOUT, U_FIN, U_OUT),
    (),
    (U_FOUT,),
    (),
    (U_FIN,),
    (U_FOUT, U_OUT, U_QKV0, U_QKV1),
    (),
    (U_FIN,),
    (U_OUT, U_POINT0),
    (U_QKV0, U_POINT1),
    (),
    (U_QKV1, U_FOUT),
    (),
    (),
    (U_QKV0,),
    (U_POINT0,),
    (U_QKV1,),
    (U_FIN,),
    (),
    (U_OUT, U_POINT1),
    (U_FOUT, U_POINT0),
    (U_QKV0,),
    (U_LEFT0, U_LEFT1, U_QKV1),
    (U_POINT1, U_CONV),
    (),
    (U_POINT0, U_FIN),
    (),
    (U_OUT, U_GLU0),
)
TAIL = (
    (U_GLU1, U_LEFT0, SMALL, U_QKV0, U_POINT1, U_LEFT1, U_QKV1, U_LEFT0, U_POINT0, U_CONV, U_LEFT1, U_POINT1, U_GLU0, U_LEFT0, U_GLU1, U_CONV, SMALL),
    (U_GLU0, U_LEFT1, U_GLU1, SMALL, U_LEFT0, U_CONV, U_GLU0, U_LEFT1, U_GLU1, SMALL, U_CONV, U_GLU0, U_GLU1, SMALL, U_FOUT, U_FIN, U_OUT, U_QKV0, U_QKV1, U_POINT0, U_POINT1, U_LEFT0, U_LEFT1, U_CONV, U_GLU0, U_GLU1, SMALL),
)

MB, MW = 128, 256
FAR = -(2.0**30)


def mm(a, b):
    return lax.dot_general(a, b, (((1,), (0,)), ((), ())), preferred_element_type=F32)


def mm_t(a, b):
    return lax.dot_general(a, b, (((1,), (1,)), ((), ())), preferred_element_type=F32)


def mm_tn(a, b):
    return lax.dot_general(a, b, (((0,), (0,)), ((), ())), preferred_element_type=F32)


def normed(v):
    centred = v - jnp.mean(v, axis=-1, keepdims=True)
    r = lax.rsqrt(jnp.mean(centred * centred, axis=-1, keepdims=True) + EPS)
    return centred * r, r


def gelu_both(v):
    c = math.sqrt(2.0 / math.pi)
    sq = v * v
    t = jnp.tanh(v * (c + (c * 0.044715) * sq))
    half = 0.5 * t + 0.5
    value = v * half
    slope = half + (0.5 * v) * (1.0 - t * t) * (c + (3.0 * c * 0.044715) * sq)
    return value, slope


def sigmoid(v):
    return 0.5 * jnp.tanh(0.5 * v) + 0.5


class Buffers:
    pass


class Plan:
    def __init__(self, dp, n, seqs, span, width, hidden, half):
        self.n, self.Z = n, dp // 2
        self.S, self.span = seqs, span
        self.D, self.FF, self.HALF = width, hidden, half
        self.LEN = span * n
        self.T = self.LEN // 2
        self.PH = n // 2
        self.B = math.isqrt(n)
        self.A = n // self.B
        assert self.A == self.B and n == 2 * seqs and dp % 2 == 0
        self.shared = SHARED if self.Z % 2 == 0 else ()
        self.sw = max(span, 128)
        self.sr = self.sw // span
        dn = width // n
        self.nw = max(dn, 128)
        self.nr = self.nw // dn
        self.FFn = hidden // n
        self.dims = [
            (width, 2 * width),
            (width, half),
            (width, hidden),
            (hidden, width),
            (width, 3 * width),
            (width, width),
            (width, hidden),
            (hidden, width),
        ]

    def whole(self, w):
        k, cols = self.dims[w]
        return (3, k, cols) if w == CONV else (k, cols)

    def kr(self, w):
        return self.dims[w][0] // self.n

    def hr(self, w):
        return self.kr(w) // 2

    def gcols(self, w):
        return self.dims[w][1] * (3 if w == CONV else 1)

    def piece(self, w, rows):
        return (rows, self.gcols(w))

    def buffers(self, take):
        T, D, FF, H, n = self.T, self.D, self.FF, self.HALF, self.n
        r = Buffers()

        def vm(shape, dtype):
            return take(pltpu.VMEM(shape, dtype))

        def sem(*shape):
            return take(pltpu.SemaphoreType.DMA(shape))

        every = range(WEIGHTS)
        parts = [(self.piece(w, self.hr(w)), BF16) for w in every] + [((16, FF // 2), BF16)]
        r.w = [vm(self.whole(w), BF16) for w in every]
        r.g8 = vm((16, FF), F32)
        r.gsm = vm((32, FF // 2), BF16)
        r.r = [None] * WEIGHTS + [vm((16, FF // 2), BF16)]
        for w in (CONV, QKV, OUT, FIN, FOUT):
            r.r[w] = vm(self.piece(w, n * self.hr(w)), BF16)
        r.r[LEFT], r.r[POINT], r.r[GLU] = r.r[FIN], r.r[FOUT], r.r[QKV]
        r.p = [vm((n - 1,) + shape, dtype) for shape, dtype in parts]
        if self.Z > 1:
            r.u = [vm(shape, dtype) for shape, dtype in parts]
            r.d = [vm(shape, dtype) for shape, dtype in parts]
        r.segbuf = vm((n, 8, self.sw), F32)
        r.segrow = vm((8, self.LEN), F32)
        r.segcol = vm((self.LEN + 16, 128), F32)
        r.segloc = vm((T + 16, 128), F32)
        r.mext = vm((T + 16, 128), F32)
        r.ms = vm((T // MB, 9 * MB, MW), BF16)
        r.qenc = vm((T, 128), BF16)
        r.kenc = vm((self.LEN, 128), BF16)
        r.smallbuf = vm((n, 32, self.FFn), BF16)
        r.nrm = vm((8, D), F32)
        r.midp = vm((16, FF), F32)
        r.xin = vm((T, D), BF16)
        r.cot = vm((T, D), BF16)
        r.a1 = vm((T, D), BF16)
        r.sg = vm((T, 2 * D), BF16)
        r.y1 = vm((T, D), F32)
        r.a2 = vm((T, D), BF16)
        r.pext = vm((3, T + 16, H), F32)
        r.dgl = vm((T, FF), BF16)
        r.dgr = vm((T, H), BF16)
        r.nm = vm((T, FF), BF16)
        r.rm = vm((T, 1), F32)
        r.big = vm((T + 16, FF), F32)
        r.sep = vm((T, FF), BF16)
        r.y2 = vm((T, D), F32)
        r.a4 = vm((T, D), BF16)
        r.qb = vm((T, D), BF16)
        r.kvb = vm((self.LEN, 2 * D), BF16)
        r.lse = vm((T, 128), F32)
        r.ctx = vm((T, D), BF16)
        r.y3 = vm((T, D), F32)
        r.a5 = vm((T, D), BF16)
        r.hid = vm((T + 32, FF), BF16)
        r.dg = vm((T, FF), BF16)
        r.osend = vm((T, D), BF16)
        r.gs = r.y3
        r.dkvr = vm((T, 2 * D), BF16)
        r.tr = vm((D, T), BF16)
        edges = (((8, H), F32), ((16, FF), BF16), ((16, FF), BF16), ((8, H), F32))
        r.es = [vm(shape, dtype) for shape, dtype in edges]
        r.er = [vm(shape, dtype) for shape, dtype in edges]
        r.s_loc = sem(WEIGHTS)
        r.s_as = sem(WEIGHTS)
        r.s_ar = sem(WEIGHTS, self.B - 1)
        r.s_br = sem(WEIGHTS, (self.A - 1) * self.B)
        r.s_ds = sem(WEIGHTS)
        r.s_dr = sem(WEIGHTS)
        if self.shared:
            r.s_hs = sem(WEIGHTS)
            r.s_hr = sem(WEIGHTS)
        r.s_rs = sem(UNITS)
        r.s_rr = sem(UNITS)
        r.s_ps = sem(UNITS, 2)
        r.s_pr = sem(UNITS, 2)
        if self.Z > 1:
            r.s_zs = sem(UNITS, 2)
            r.s_zr = sem(UNITS, 2)
        r.s_fs = sem(UNITS)
        r.s_fr = sem(UNITS)
        r.s_fl = sem(UNITS)
        r.s_xs = sem(4, self.S)
        r.s_xr = sem(4, max(self.PH, self.S))
        r.s_gs = sem(2 * self.S)
        r.s_gr = sem(n)
        r.s_ms = sem(n)
        r.s_mr = sem(n)
        r.s_es = sem(4)
        r.s_er = sem(4)
        r.s_ks = sem(1)
        r.s_kr = sem(1)
        r.s_js = sem(HEADS // 2)
        r.s_jr = sem(HEADS // 2)
        return r


INPUTS = 4 + WEIGHTS
OUTPUTS = 2 + WEIGHTS + 1


def kernel(plan, *refs):
    ins, outs = refs[:INPUTS], refs[INPUTS : INPUTS + OUTPUTS]
    scratch = iter(refs[INPUTS + OUTPUTS :])
    r = plan.buffers(lambda shape: next(scratch))
    r.x, r.seg, r.ct, r.small = ins[:4]
    r.h = ins[4:]
    r.o_out, r.o_ig = outs[:2]
    r.o = outs[2:]
    n, Z, S, span = plan.n, plan.Z, plan.S, plan.span
    T, D, FF, H, PH = plan.T, plan.D, plan.FF, plan.HALF, plan.PH
    A, B = plan.A, plan.B
    dp, q = lax.axis_index("dp"), lax.axis_index("seq")
    z, c = dp // 2, dp % 2
    oc = 1 - c

    def aligned(v, m=16):
        return pl.multiple_of(v, m)

    def dev(core, chip, plane=None):
        return ((z if plane is None else plane) * 2 + core, chip)

    sibling = dev(oc, q)

    def remote(src, dst, ss, rs, to):
        return pltpu.make_async_remote_copy(
            src_ref=src, dst_ref=dst, send_sem=ss, recv_sem=rs, device_id=to, device_id_type=MESH
        )

    barrier = pltpu.get_barrier_semaphore()
    for core in range(2):

        def greet(t, _, core=core):
            chip = lax.rem(q + t, n)
            to = (z * 2 + (c + core) % 2, chip)
            pl.semaphore_signal(barrier, inc=1, device_id=to, device_id_type=MESH)
            return 0

        lax.fori_loop(1 - core, n, greet, 0)
    if Z > 1:

        @pl.when(z > 0)
        def _():
            pl.semaphore_signal(barrier, inc=1, device_id=dev(c, q, z - 1), device_id_type=MESH)

        @pl.when(z < Z - 1)
        def _():
            pl.semaphore_signal(barrier, inc=1, device_id=dev(c, q, z + 1), device_id_type=MESH)

    pl.semaphore_wait(barrier, 2 * n - 1 + (z + Z - 1) // Z + (2 * Z - 2 - z) // Z)

    def vrows(ref, w, row0, rows):
        ds = pl.ds(aligned(row0), rows)
        return ref.at[:, ds] if w == CONV else ref.at[ds]

    def bytes_of(view, semaphore):
        return pltpu.make_async_copy(view, view, semaphore)

    def qof(core, f, g):
        f, g = f % B, g % B
        return core * (f * B + g) + (1 - core) * (g * B + f)

    b_, a_ = q % B, q // B
    f_, g_ = c * a_ + oc * b_, c * b_ + oc * a_
    par = z % 2
    partner = dev(c, q, z + 1 - 2 * par)

    def wrows(ref, w, row0, rows, side):
        if w not in plan.shared:
            return vrows(ref, w, row0, rows)
        size = plan.dims[w][1] // 2
        cols = pl.ds(pl.multiple_of(side * size, 128), size)
        if w == CONV:
            return ref.at[:, pl.ds(aligned(row0), rows), cols]
        return ref.at[pl.ds(aligned(row0), rows), cols]

    def wblock(w, shard, side=par):
        return wrows(r.w[w], w, shard * plan.kr(w) + c * plan.hr(w), plan.hr(w), side)

    def own_block(w):
        return wrows(r.h[w], w, c * plan.hr(w), plan.hr(w), par)

    def copy_a(w, t):
        to = dev(c, qof(c, f_ + t, g_))
        return remote(own_block(w), wblock(w, q), r.s_as.at[w], r.s_ar.at[w, t - 1], to)

    def copy_b(w, u, t):
        blk = wblock(w, qof(c, f_ + B - t, g_))
        src = own_block(w) if t == 0 else blk
        to = dev(c, qof(c, f_, g_ + u))
        return remote(src, blk, r.s_as.at[w], r.s_br.at[w, (u - 1) * B + t], to)

    def shard_from(u, t):
        return qof(c, f_ + B - t, g_ + B - u)

    def pass_on(w, u, t):
        blk = wblock(w, shard_from(u, t))
        remote(blk, blk, r.s_ds.at[w], r.s_dr.at[w], sibling).start()
        if w in plan.shared:
            remote(blk, blk, r.s_hs.at[w], r.s_hr.at[w], partner).start()

    def local_shard(w):
        dst = vrows(r.w[w], w, q * plan.kr(w), plan.kr(w))
        return pltpu.make_async_copy(r.h[w], dst, r.s_loc.at[w])

    def g0(w):
        local_shard(w).start()
        for t in range(1, B):
            copy_a(w, t).start()
        for u in range(1, A):
            copy_b(w, u, 0).start()

    def g1(w):
        for t in range(1, B):
            bytes_of(wblock(w, shard_from(0, t)), r.s_ar.at[w, t - 1]).wait()
            for u in range(1, A):
                copy_b(w, u, t).start()
            pass_on(w, 0, t)

    def g2(w):
        for u in range(1, A):
            for t in range(B):
                bytes_of(wblock(w, shard_from(u, t)), r.s_br.at[w, (u - 1) * B + t]).wait()
                pass_on(w, u, t)

    def others(w):
        return wrows(r.w[w], w, 0, (n - 1) * plan.hr(w), 0)

    def gz(w):
        if w not in plan.shared:
            return
        bytes_of(others(w), r.s_hr.at[w]).wait()
        for u in range(A):
            for t in range(B):
                if (u, t) != (0, 0):
                    blk = wblock(w, shard_from(u, t), 1 - par)
                    remote(blk, blk, r.s_ds.at[w], r.s_dr.at[w], sibling).start()

    def g3(w):
        local_shard(w).wait()
        bytes_of(vrows(r.w[w], w, 0, (n - 1) * plan.hr(w)), r.s_dr.at[w]).wait()

    gather_steps = (g0, g1, g2, gz)
    forward_turns = iter(FORWARD)

    def gather(steps):
        for k, w in steps:
            if w == TOKENS:
                tokens_in(r.ct, r.cot, 1)
            else:
                gather_steps[k](w)

    def pass_turn():
        gather(next(forward_turns))

    def pass_turns(count):
        every = [(k, next(forward_turns)) for k in range(count)]
        return [(k, lambda steps=steps: gather(steps)) for k, steps in every if steps]

    def gather_sent(w):
        bytes_of(others(w), r.s_as.at[w]).wait()
        bytes_of(vrows(r.w[w], w, 0, (n - 1) * plan.hr(w)), r.s_ds.at[w]).wait()
        if w in plan.shared:
            bytes_of(others(w), r.s_hs.at[w]).wait()

    def token_rows(ref, slot):
        return ref.at[pl.ds(aligned(slot * span), span)]

    def tokens_in(src, dst, k):
        for j in range(S):
            chip, core, slot = S * c + j, q // PH, q % PH
            here = jnp.logical_and(chip == q, core == c)
            there = token_rows(dst, slot)

            @pl.when(here)
            def _():
                pltpu.make_async_copy(src.at[j], there, r.s_xr.at[k, slot]).start()

            @pl.when(jnp.logical_not(here))
            def _():
                remote(
                    src.at[j], there, r.s_xs.at[k, j], r.s_xr.at[k, slot], dev(core, chip)
                ).start()

    def tokens_in_done(dst, k):
        for slot in range(PH):
            blk = token_rows(dst, slot)
            pltpu.make_async_copy(blk, blk, r.s_xr.at[k, slot]).wait()

    def tokens_in_sent(src, dst, k):
        for j in range(S):
            chip, core, slot = S * c + j, q // PH, q % PH
            here = jnp.logical_and(chip == q, core == c)

            @pl.when(jnp.logical_not(here))
            def _():
                remote(
                    src.at[j],
                    token_rows(dst, slot),
                    r.s_xs.at[k, j],
                    r.s_xr.at[k, slot],
                    dev(core, chip),
                ).wait_send()

    def tokens_out(src, dst, k):
        for p in range(PH):
            chip, core, slot = c * PH + p, q // S, q % S
            here = jnp.logical_and(chip == q, core == c)

            @pl.when(here)
            def _():
                pltpu.make_async_copy(token_rows(src, p), dst.at[slot], r.s_xr.at[k, slot]).start()

            @pl.when(jnp.logical_not(here))
            def _():
                remote(
                    token_rows(src, p),
                    dst.at[slot],
                    r.s_xs.at[k, p],
                    r.s_xr.at[k, slot],
                    dev(core, chip),
                ).start()

    def tokens_out_done(src, dst, k):
        for j in range(S):
            pltpu.make_async_copy(dst.at[j], dst.at[j], r.s_xr.at[k, j]).wait()
        for p in range(PH):
            chip, core, slot = c * PH + p, q // S, q % S
            here = jnp.logical_and(chip == q, core == c)

            @pl.when(jnp.logical_not(here))
            def _():
                remote(
                    token_rows(src, p),
                    dst.at[slot],
                    r.s_xs.at[k, p],
                    r.s_xr.at[k, slot],
                    dev(core, chip),
                ).wait_send()

    def seg_send():
        for j in range(S):
            for core in range(2):
                chip = S * c + j
                here = jnp.logical_and(chip == q, c == core)
                i = 2 * j + core

                @pl.when(here)
                def _():
                    pltpu.make_async_copy(r.seg.at[j], r.segbuf.at[q], r.s_gr.at[q]).start()

                @pl.when(jnp.logical_not(here))
                def _():
                    remote(
                        r.seg.at[j],
                        r.segbuf.at[q],
                        r.s_gs.at[i],
                        r.s_gr.at[q],
                        dev(core, chip),
                    ).start()

    def seg_sent():
        for j in range(S):
            for core in range(2):
                chip = S * c + j
                here = jnp.logical_and(chip == q, c == core)

                @pl.when(jnp.logical_not(here))
                def _():
                    remote(
                        r.seg.at[j],
                        r.segbuf.at[q],
                        r.s_gs.at[2 * j + core],
                        r.s_gr.at[q],
                        dev(core, chip),
                    ).wait_send()

    def small_copy(t):
        return remote(
            r.small,
            r.smallbuf.at[q],
            r.s_ms.at[t],
            r.s_mr.at[t],
            dev(c, (q + t) % n),
        )

    def small_arrived(t):
        blk = r.smallbuf.at[(q + n - t) % n]
        return remote(blk, blk, r.s_ms.at[t], r.s_mr.at[t], sibling)

    def edge_copy(i):
        return remote(r.es[i], r.er[i], r.s_es.at[i], r.s_er.at[i], sibling)

    def edge_send(i, last, first):
        r.es[i][...] = jnp.where(c == 0, last, first)
        edge_copy(i).start()

    def edge_take(i):
        edge_copy(i).wait()
        got = r.er[i][...]
        none = jnp.zeros_like(got)
        return jnp.where(c == 1, got, none), jnp.where(c == 0, got, none)

    def columns(u):
        w, half = UNIT_WEIGHT[u], UNIT_PART[u]
        size = plan.gcols(w)
        return (0, size) if half is None else (half * (size // 2), size // 2)

    def urows(ref, u, row0, rows, shift=0):
        col0, size = columns(u)
        return ref.at[pl.ds(aligned(row0), rows), pl.ds(col0 + shift, size)]

    grad_home = {GLU: (r.hid, 2 * D), CONV: (r.dkvr, 0), LEFT: (r.sep, 0), QKV: (r.dg, 0)}

    def gpiece(u, shard, half):
        if u == SMALL:
            return r.gsm.at[pl.ds(pl.multiple_of(half * 16, 16), 16)]
        w = UNIT_WEIGHT[u]
        ref, shift = grad_home.get(w, (r.w[w] if w < WEIGHTS else None, 0))
        return urows(ref, u, shard * plan.kr(w) + half * plan.hr(w), plan.hr(w), shift)

    def rpiece(u, shard):
        w = UNIT_WEIGHT[u]
        if u == SMALL:
            return r.r[w]
        return urows(r.r[w], u, shard * plan.hr(w), plan.hr(w))

    def slots(u, first, count):
        buf = r.p[UNIT_WEIGHT[u]]
        if u == SMALL:
            return buf.at[pl.ds(first, count)]
        col0, size = columns(u)
        return buf.at[pl.ds(first, count), :, pl.ds(col0, size)]

    def ppiece(u, slot):
        buf = r.p[UNIT_WEIGHT[u]]
        if u == SMALL:
            return buf.at[slot]
        col0, size = columns(u)
        return buf.at[slot, :, pl.ds(col0, size)]

    def zpiece(u, way):
        buf = (r.u, r.d)[way][UNIT_WEIGHT[u]]
        if u == SMALL:
            return buf
        col0, size = columns(u)
        return buf.at[:, pl.ds(col0, size)]

    def copy_r(u, s):
        return remote(gpiece(u, s, oc), rpiece(u, s), r.s_rs.at[u], r.s_rr.at[u], sibling)

    def all_r(u, semaphore):
        w = UNIT_WEIGHT[u]
        view = r.r[w] if u == SMALL else urows(r.r[w], u, 0, n * plan.hr(w))
        return bytes_of(view, semaphore.at[u])

    def shards(u):
        return 1 if u == SMALL else n

    def red0(u):
        for s in range(shards(u)):
            copy_r(u, s).start()

    def plus(a, b):
        return a[...].astype(F32) + b[...].astype(F32)

    def add_core(u, s):
        mine = gpiece(u, s, c)
        mine[...] = plus(mine, rpiece(u, s)).astype(mine.dtype)

    def slot1(u, t):
        return (u - 1) * B + t

    def slot2(t):
        return (A - 1) * B + t - 1

    def copy_p1(u, k, t):
        return remote(
            gpiece(u, qof(c, f_ + t, g_ + k), c),
            ppiece(u, slot1(k, t)),
            r.s_ps.at[u, 0],
            r.s_pr.at[u, 0],
            dev(c, qof(c, f_, g_ + k)),
        )

    def copy_p2(u, t):
        to = qof(c, f_ + t, g_)
        return remote(
            r.r[WEIGHTS] if u == SMALL else gpiece(u, to, c),
            ppiece(u, slot2(t)),
            r.s_ps.at[u, 1],
            r.s_pr.at[u, 1],
            dev(c, to),
        )

    def all_p(u, step, semaphore):
        count = B - 1 if step else A - 1 if u == SMALL else (A - 1) * B
        return bytes_of(slots(u, 0, count), semaphore.at[u, step])

    def red1(u):
        all_r(u, r.s_rr).wait()
        if u == SMALL:
            add_core(u, 0)
            for k in range(1, A):
                copy_p1(u, k, 0).start()
            return

        def send(i, _):
            k, t = i // B + 1, i % B
            add_core(u, qof(c, f_ + t, g_ + k))
            copy_p1(u, k, t).start()
            return 0

        lax.fori_loop(0, (A - 1) * B, send, 0)
        lax.fori_loop(0, B, lambda t, _: (add_core(u, qof(c, f_ + t, g_)), 0)[1], 0)

    def red1b(u):
        all_p(u, 0, r.s_pr).wait()

        def send(t, _):
            if u == SMALL:
                total, to = gpiece(u, 0, c)[...].astype(F32), r.r[WEIGHTS]
            else:
                to = gpiece(u, qof(c, f_ + t, g_), c)
                total = to[...].astype(F32)
            for k in range(1, A):
                total = total + ppiece(u, slot1(k, 0 if u == SMALL else t))[...].astype(F32)
            to[...] = total.astype(to.dtype)
            if u != SMALL:
                copy_p2(u, t).start()
            return 0

        if u == SMALL:
            send(0, 0)
            for t in range(1, B):
                copy_p2(u, t).start()
        else:
            lax.fori_loop(1, B, send, 0)

    def red2(u):
        all_p(u, 1, r.s_pr).wait()
        total = (r.r[WEIGHTS] if u == SMALL else gpiece(u, q, c))[...].astype(F32)
        if u != SMALL:
            for k in range(1, A):
                total = total + ppiece(u, slot1(k, 0))[...].astype(F32)
        for t in range(1, B):
            total = total + ppiece(u, slot2(t))[...].astype(F32)
        mine = ppiece(u, 0)
        mine[...] = total.astype(mine.dtype)

    def copy_z(u, way):
        return remote(
            ppiece(u, 1 + way),
            zpiece(u, way),
            r.s_zs.at[u, way],
            r.s_zr.at[u, way],
            dev(c, q, z + 1 if way == 0 else z - 1),
        )

    def red_hop(u, h):
        own, up, down = ppiece(u, 0), ppiece(u, 1), ppiece(u, 2)

        @pl.when(z == h)
        def _():
            if h == 0:
                up[...] = own[...]
            else:
                copy_z(u, 0).wait_recv()
                up[...] = plus(own, zpiece(u, 0)).astype(up.dtype)
            if h < Z - 1:
                copy_z(u, 0).start()

        @pl.when(z == Z - 1 - h)
        def _():
            if h == 0:
                down[...] = own[...]
            else:
                copy_z(u, 1).wait_recv()
                if h < Z - 1:
                    down[...] = plus(own, zpiece(u, 1)).astype(down.dtype)
            if h < Z - 1:
                copy_z(u, 1).start()

    def final_rows(u):
        w = UNIT_WEIGHT[u]
        if u == SMALL:
            return r.o[w].at[pl.ds(pl.multiple_of(c * 16, 16), 16)]
        return urows(r.o[w], u, c * plan.hr(w), plan.hr(w))

    def final_local(u):
        return pltpu.make_async_copy(ppiece(u, 0), final_rows(u), r.s_fl.at[u])

    def final_remote(u):
        return remote(ppiece(u, 0), final_rows(u), r.s_fs.at[u], r.s_fr.at[u], sibling)

    def red_final(u):
        if Z > 1:
            own, up = ppiece(u, 0), ppiece(u, 1)

            @pl.when(z == Z - 1)
            def _():
                own[...] = up[...]

            @pl.when(z < Z - 1)
            def _():
                own[...] = plus(up, zpiece(u, 1)).astype(own.dtype)

        final_local(u).start()
        final_remote(u).start()

    def red_end(u):
        final_local(u).wait()
        final_remote(u).wait()
        all_r(u, r.s_rs).wait()
        all_p(u, 0, r.s_ps).wait()
        all_p(u, 1, r.s_ps).wait()
        if Z > 1:

            @pl.when(z < Z - 1)
            def _():
                copy_z(u, 0).wait_send()

            @pl.when(z > 0)
            def _():
                copy_z(u, 1).wait_send()

    def red2_hop(u):
        red2(u)
        red_hop(u, 0)

    def last_hop(u):
        red_hop(u, Z - 1)
        red_final(u)

    ahead = {}
    turns = iter(SCHEDULE)

    def enlist(u):
        if Z > 1:
            ahead[u] = [red1, red1b, red2_hop]
            ahead[u] += [lambda k, h=h: red_hop(k, h) for h in range(1, Z - 1)]
            ahead[u].append(last_hop)
        else:
            ahead[u] = [red1, red1b, red2, red_final]

    def reduce_start(*units):
        for u in units:
            red0(u)
            enlist(u)

    def steps_of(units):
        return [(ahead[u].pop(0), u) for u in units if ahead[u]]

    def move(units):
        for step, u in steps_of(units):
            step(u)

    def turn():
        move(next(turns))

    def turns_of(count):
        acts = []
        for k in range(count):
            steps = steps_of(next(turns))
            if steps:
                acts.append((k, lambda steps=steps: [step(u) for step, u in steps][:0]))
        return acts

    def loop(count, body, after=()):
        def step(i, _):
            body(i)
            for k, act in after:
                pl.when(i == k)(lambda act=act: (act(), None)[1])
            return 0

        lax.fori_loop(0, count, step, 0)

    RB = 256
    NB = T // RB

    def rows_of(i, size=RB, base=0):
        return pl.ds(pl.multiple_of(i * size + base, base or size), size)

    seg_send()
    small_local = pltpu.make_async_copy(r.small, r.smallbuf.at[q], r.s_mr.at[0])
    small_local.start()
    for what in START:
        if what == SMALLS:
            for t in range(1, n):
                small_copy(t).start()
        elif what == TOKENS:
            tokens_in(r.x, r.xin, 0)
        else:
            g0(what)
    r.g8[...] = jnp.zeros((16, FF), F32)
    pass_turn()

    for s in range(n):
        blk = r.segbuf.at[s]
        pltpu.make_async_copy(blk, blk, r.s_gr.at[s]).wait()
    for grp in range(n // plan.sr):
        got = r.segbuf[grp * plan.sr]
        for k in range(1, plan.sr):
            got = got + r.segbuf[grp * plan.sr + k]
        r.segrow[:, grp * plan.sw : (grp + 1) * plan.sw] = got
    r.segcol[0:8] = jnp.full((8, 128), -1.0, F32)
    r.segcol[plan.LEN + 8 : plan.LEN + 16] = jnp.full((8, 128), -1.0, F32)
    for k in range(plan.LEN // 128):
        row = r.segrow[0:1, k * 128 : (k + 1) * 128]
        r.segcol[8 + k * 128 : 8 + (k + 1) * 128] = jnp.broadcast_to(row, (128, 128)).T
    r.segloc[...] = r.segcol[pl.ds(pl.multiple_of(c * T, 8), T + 16)]
    r.mext[0 : T + 8] = jnp.where(r.segloc[0 : T + 8] == r.segloc[1 : T + 9], 1.0, 0.0)

    def mask(o, start, rows):
        first = 8 + start + (0 if o > 0 else o)
        return r.mext[first : first + rows]

    small_local.wait()
    for t in range(1, n):
        small_arrived(t).wait_recv()
    for grp in range(n // plan.nr):
        got = r.smallbuf[grp * plan.nr].astype(F32)[0:8, 0 : plan.nw]
        for k in range(1, plan.nr):
            got = got + r.smallbuf[grp * plan.nr + k].astype(F32)[0:8, 0 : plan.nw]
        r.nrm[:, grp * plan.nw : (grp + 1) * plan.nw] = got
    for s in range(n):
        r.midp[:, s * plan.FFn : (s + 1) * plan.FFn] = r.smallbuf[s].astype(F32)[8:24]

    def ln_out(k, v):
        unit, _ = normed(v)
        return (unit * r.nrm[k : k + 1] + r.nrm[4 + k : 5 + k]).astype(BF16)

    def ln_back(k, e, v):
        unit, rs = normed(v)
        eg = e * r.nrm[k : k + 1]
        m1 = jnp.mean(eg, axis=-1, keepdims=True)
        m2 = jnp.mean(eg * unit, axis=-1, keepdims=True)
        cols = slice(k * D, (k + 1) * D)
        r.g8[11:12, cols] += jnp.sum(e * unit, axis=0, keepdims=True)
        r.g8[12:13, cols] += jnp.sum(e, axis=0, keepdims=True)
        return rs * (eg - m1 - unit * m2)

    pass_turn()

    def window(b):
        return min(max(b * MB - (MW - MB) // 2 + 16, 0), T + 32 - MW)

    ahead_of = lax.broadcasted_iota(jnp.int32, (MB, MW), 1) - lax.broadcasted_iota(
        jnp.int32, (MB, MW), 0
    )
    for b in range(T // MB):
        home = r.segloc[8 + b * MB : 8 + (b + 1) * MB]
        for o in range(-4, 5):
            there = r.segloc[8 + b * MB + o : 8 + (b + 1) * MB + o]
            same = jnp.where(home == there, 1.0, 0.0)
            hit = ahead_of == b * MB + 16 - window(b) + o
            tap = jnp.where(hit, jnp.concatenate([same] * (MW // 128), axis=1), 0.0)
            r.ms[b, (o + 4) * MB : (o + 5) * MB] = tap.astype(BF16)

    lane = lax.broadcasted_iota(jnp.int32, (1, 128), 1)
    lane_f = lane.astype(F32)
    own_doc = r.segloc[8 : T + 8] == lane_f
    r.qenc[...] = jnp.where(jnp.logical_and(lane < 4, jnp.logical_not(own_doc)), FAR, 0.0).astype(BF16)
    ones = jnp.logical_and(lane >= 4, lane < 7)
    r.kenc[...] = jnp.where(
        jnp.logical_or(r.segcol[8 : plan.LEN + 8] == lane_f, ones), 1.0, 0.0
    ).astype(BF16)

    pass_turn()
    pass_turn()
    g3(GLU)
    pass_turn()
    tokens_in_done(r.xin, 0)

    def glu(i):
        rows = rows_of(i)
        x = r.xin[rows].astype(F32)
        a1 = ln_out(0, x)
        r.a1[rows] = a1
        value = mm(a1, r.w[GLU][:, 0:D])
        gate = sigmoid(mm(a1, r.w[GLU][:, D : 2 * D]))
        r.sg[rows, 0:D] = gate.astype(BF16)
        r.sg[rows, D : 2 * D] = (value * gate * (1.0 - gate)).astype(BF16)
        y1 = x + value * gate
        r.y1[rows] = y1
        r.a2[rows] = ln_out(1, y1)

    loop(NB, glu, pass_turns(NB))
    pass_turn()
    g3(CONV)

    def conv(i):
        a2 = r.a2[rows_of(i)]
        for o in range(3):
            r.pext[o, rows_of(i, RB, 8)] = mm(a2, r.w[CONV][o])

    loop(NB, conv)
    edge_send(0, r.pext[0, T : T + 8], r.pext[2, 8:16])
    pass_turn()
    top, bottom = edge_take(0)
    r.pext[0, 0:8] = top
    r.pext[2, T + 8 : T + 16] = bottom
    pass_turn()
    for k in range(T // 128):
        lo = k * 128
        before = mask(-1, lo, 128)
        after = mask(1, lo, 128)
        pre = (
            r.pext[0, lo + 7 : lo + 135] * jnp.concatenate([before] * (H // 128), axis=1)
            + r.pext[1, lo + 8 : lo + 136]
            + r.pext[2, lo + 9 : lo + 137] * jnp.concatenate([after] * (H // 128), axis=1)
        )
        value, slope = gelu_both(pre)
        r.pext[1, lo + 8 : lo + 136] = value
        r.dgr[lo : lo + 128] = slope.astype(BF16)
    pass_turn()
    pass_turn()
    g3(LEFT)

    CH = 512
    RM = 128

    def left(i):
        rows, erows = rows_of(i, RM), rows_of(i, RM, 8)
        a2 = r.a2[rows]
        for k in range(FF // CH):
            value, slope = gelu_both(mm(a2, r.w[LEFT][:, k * CH : (k + 1) * CH]))
            r.dgl[rows, k * CH : (k + 1) * CH] = slope.astype(BF16)
            r.big[erows, k * CH : (k + 1) * CH] = value
        r.big[erows, 0:H] += r.pext[1, erows]
        unit, rs = normed(r.big[erows])
        r.nm[rows] = unit.astype(BF16)
        r.rm[rows] = rs
        r.hid[rows_of(i, RM, 16)] = (unit * r.midp[0:1] + r.midp[1:2]).astype(BF16)

    loop(T // RM, left, pass_turns(T // RM))
    edge_send(1, r.hid[T : T + 16], r.hid[16:32])
    r.hid[0:16], r.hid[T + 16 : T + 32] = edge_take(1)
    pass_turn()

    def depthwise(j):
        cols = pl.ds(pl.multiple_of(j * 256, 256), 256)
        for b in range(T // MB):
            near = r.hid[window(b) : window(b) + MW, cols]
            taps = mm(r.ms[b], near)
            total = taps[0:MB] * r.midp[2:3, cols]
            for o in range(1, 9):
                total = total + taps[o * MB : (o + 1) * MB] * r.midp[2 + o : 3 + o, cols]
            r.sep[b * MB : (b + 1) * MB, cols] = total.astype(BF16)

    loop(FF // 256, depthwise, pass_turns(FF // 256))
    pass_turn()
    g3(POINT)

    def point(i):
        rows = rows_of(i)
        y2 = r.y1[rows] + mm(r.sep[rows], r.w[POINT][...])
        r.y2[rows] = y2
        r.a4[rows] = ln_out(2, y2)

    loop(NB, point)
    pass_turn()
    pass_turn()
    g3(QKV)
    scale = 1.0 / math.sqrt(D // HEADS)

    def qkv(i):
        rows = rows_of(i)
        a4 = r.a4[rows]
        r.qb[rows] = (mm(a4, r.w[QKV][:, 0:D]) * scale).astype(BF16)
        here = pl.ds(pl.multiple_of(c * T + i * RB, RB), RB)
        r.kvb[here, 0:D] = mm(a4, r.w[QKV][:, D : 2 * D]).astype(BF16)
        r.kvb[here, D : 2 * D] = mm(a4, r.w[QKV][:, 2 * D : 3 * D]).astype(BF16)

    loop(NB, qkv)

    def kv_copy():
        blk = r.kvb.at[pl.ds(aligned(c * T), T)]
        return remote(blk, blk, r.s_ks.at[0], r.s_kr.at[0], sibling)

    kv_copy().start()
    pass_turn()
    heads_lanes = [lane < 64, lane >= 64]
    kv_copy().wait()
    pass_turn()

    def pair_cols(j, base=0):
        return pl.ds(pl.multiple_of(j * 128 + base, 128), 128)

    def head_lanes(e, v):
        return jnp.where(heads_lanes[e], v, jnp.zeros_like(v))

    def attend(j):
        cols, vcols = pair_cols(j), pair_cols(j, D)
        keys = jnp.concatenate([r.kvb[:, cols], r.kenc[...]], axis=1)
        for k in range(T // RB):
            rows = slice(k * RB, (k + 1) * RB)
            q2 = r.qb[rows, cols]
            got = []
            for e in range(2):
                score = mm_t(jnp.concatenate([head_lanes(e, q2), r.qenc[rows]], axis=1), keys)
                most = jnp.max(score, axis=-1, keepdims=True)
                power = jnp.exp(score - most)
                total = jnp.sum(power, axis=-1, keepdims=True)
                got.append(mm(power.astype(BF16), r.kvb[:, vcols]) / total)
                lse = most + jnp.log(total)
                r.lse[rows] = jnp.where(lane == 2 * j + e, lse, r.lse[rows])
            r.ctx[rows, cols] = jnp.where(heads_lanes[0], got[0], got[1]).astype(BF16)

    r.lse[...] = jnp.zeros((T, 128), F32)

    loop(HEADS // 2, attend, pass_turns(HEADS // 2))
    pass_turn()
    g3(OUT)

    def out(i):
        rows = rows_of(i)
        y3 = r.y2[rows] + mm(r.ctx[rows], r.w[OUT][...])
        r.y3[rows] = y3
        r.a5[rows] = ln_out(3, y3)

    loop(NB, out)
    pass_turn()
    pass_turn()
    g3(FIN)

    def ffn_in(i):
        rows = rows_of(i)
        a5 = r.a5[rows]
        for k in range(FF // CH):
            value, slope = gelu_both(mm(a5, r.w[FIN][:, k * CH : (k + 1) * CH]))
            r.hid[rows, k * CH : (k + 1) * CH] = value.astype(BF16)
            r.dg[rows, k * CH : (k + 1) * CH] = slope.astype(BF16)

    loop(NB, ffn_in, pass_turns(NB))
    pass_turn()
    g3(FOUT)

    def ffn_out(i):
        rows = rows_of(i)
        r.osend[rows] = (r.y3[rows] + mm(r.hid[rows], r.w[FOUT][...])).astype(BF16)

    loop(NB, ffn_out)
    pass_turn()
    tokens_out(r.osend, r.o_out, 2)
    for w in range(WEIGHTS):
        gather_sent(w)

    tokens_in_done(r.cot, 1)

    def ffn_back(i):
        rows = rows_of(i)
        f4 = r.cot[rows]
        for k in range(FF // CH):
            cols = slice(k * CH, (k + 1) * CH)
            up = mm_t(f4, r.w[FOUT][cols])
            r.dg[rows, cols] = (up * r.dg[rows, cols].astype(F32)).astype(BF16)
        e = mm_t(r.dg[rows], r.w[FIN][...])
        r.gs[rows] = f4.astype(F32) + ln_back(3, e, r.y3[rows])

    loop(NB, ffn_back)
    GC = 1024

    def grad_outer(k):
        cols = rows_of(k, GC)
        r.w[FOUT][cols] = mm_tn(r.hid[0:T, cols], r.cot[...]).astype(BF16)

    loop(FF // GC, grad_outer)
    reduce_start(U_FOUT)
    turn()
    r.tr[...] = r.a5[...].T

    def grad_inner(k):
        cols = rows_of(k, GC)
        r.w[FIN][:, cols] = mm(r.tr[...], r.dg[:, cols]).astype(BF16)

    loop(FF // GC, grad_inner)
    reduce_start(U_FIN)
    turn()

    def out_back(i):
        rows = rows_of(i)
        f3 = r.gs[rows].astype(BF16)
        r.a5[rows] = f3
        r.hid[rows, 3 * D : 4 * D] = mm_t(f3, r.w[OUT][...]).astype(BF16)

    loop(NB, out_back)
    r.w[OUT][...] = mm_tn(r.ctx[...], r.a5[...]).astype(BF16)
    reduce_start(U_OUT)
    turn()
    r.tr[...] = r.a4[...].T

    QB = 256

    def with_terms(extra, v):
        high = v.astype(BF16).astype(F32)
        mid = (v - high).astype(BF16).astype(F32)
        low = v - high - mid
        terms = jnp.where(lane == 4, high, jnp.where(lane == 5, mid, jnp.where(lane == 6, low, 0.0)))
        return extra - terms.astype(BF16)

    def attend_back(j):
        cols, vcols = pair_cols(j), pair_cols(j, D)
        k2 = r.kvb[:, cols]
        keys = jnp.concatenate([k2, r.kenc[...]], axis=1)
        values = jnp.concatenate([r.kvb[:, vcols], r.kenc[...]], axis=1)
        for k in range(T // QB):
            rows = slice(k * QB, (k + 1) * QB)
            q2 = r.qb[rows, cols]
            d2 = r.hid[rows, pair_cols(j, 3 * D)]
            inner = d2.astype(F32) * r.ctx[rows, cols].astype(F32)
            dq = jnp.zeros((QB, 128), F32)
            for e in range(2):
                qe, de = head_lanes(e, q2), head_lanes(e, d2)
                lse = jnp.sum(
                    jnp.where(lane == 2 * j + e, r.lse[rows], 0.0), axis=-1, keepdims=True
                )
                delta = jnp.sum(head_lanes(e, inner), axis=-1, keepdims=True)
                shifted = mm_t(keys, jnp.concatenate([qe, with_terms(r.qenc[rows], lse)], axis=1))
                probs = jnp.exp(shifted)
                none = jnp.zeros((QB, 128), BF16)
                moved = mm_t(values, jnp.concatenate([de, with_terms(none, delta)], axis=1))
                ds = (probs * moved).astype(BF16)
                dk = mm(ds, qe)
                dv = mm(probs.astype(BF16), de)
                for kk in range(2):
                    half = slice(kk * T, (kk + 1) * T)
                    at = 2 * D + kk * 128
                    if k == 0 and e == 0:
                        r.big[0:T, at : at + 128] = dk[half]
                        r.big[0:T, at + 256 : at + 384] = dv[half]
                    else:
                        r.big[0:T, at : at + 128] += dk[half]
                        r.big[0:T, at + 256 : at + 384] += dv[half]
                dq = dq + mm_tn(ds, head_lanes(e, k2))
            r.hid[rows, cols] = (dq * scale).astype(BF16)

        def part(core, what):
            at = pl.multiple_of(2 * D + core * 128 + what * 256, 128)
            return r.big[0:T, pl.ds(at, 128)]

        for what in range(2):
            mine = pl.ds(pl.multiple_of(j * 256 + what * 128, 128), 128)
            r.big[0:T, mine] = part(c, what)
            r.cot[:, pl.ds(pl.multiple_of(lax.rem(j, 2) * 256 + what * 128, 128), 128)] = part(
                oc, what
            ).astype(BF16)
        dkv_copy(j).start()

        @pl.when(j > 0)
        def _():
            pair_back(j - 1)

    def dkv_copy(j):
        slot = lax.rem(j, 2)
        return remote(
            r.cot.at[:, pl.ds(pl.multiple_of(slot * 256, 128), 256)],
            r.dkvr.at[:, pl.ds(pl.multiple_of(j * 256, 128), 256)],
            r.s_js.at[j],
            r.s_jr.at[j],
            sibling,
        )

    def pair_back(j):
        dkv_copy(j).wait()
        both = pl.ds(pl.multiple_of(j * 256, 256), 256)
        dkv = (r.big[0:T, both] + r.dkvr[:, both].astype(F32)).astype(BF16)
        pair = jnp.concatenate([r.hid[0:T, pair_cols(j)], dkv], axis=1)
        weight = jnp.concatenate([r.w[QKV][:, pair_cols(j, base)] for base in (0, D, 2 * D)], axis=1)
        share = mm_t(pair, weight)

        @pl.when(j == 0)
        def _():
            r.big[0:T, 3 * D : 4 * D] = share

        @pl.when(j > 0)
        def _():
            r.big[0:T, 3 * D : 4 * D] += share

        grad = mm(r.tr[...], pair)
        r.dg[:, pl.ds(pl.multiple_of(j * 384, 128), 384)] = grad.astype(BF16)

    acts = turns_of(3)
    enlist(U_QKV0)
    acts += [(2, lambda: red0(U_QKV0))] + [(k + 3, act) for k, act in turns_of(1)]
    loop(HEADS // 2, attend_back, acts)
    pair_back(HEADS // 2 - 1)
    reduce_start(U_QKV1)
    turn()

    def qkv_back(i):
        rows = rows_of(i)
        r.gs[rows] += ln_back(2, r.big[rows, 3 * D : 4 * D], r.y2[rows])

    loop(NB, qkv_back)

    def point_back(i):
        rows = rows_of(i)
        f2 = r.gs[rows].astype(BF16)
        r.a4[rows] = f2
        for k in range(FF // CH):
            cols = slice(k * CH, (k + 1) * CH)
            d = mm_t(f2, r.w[POINT][cols])
            r.hid[rows_of(i, RB, 16), cols] = d.astype(BF16)

    loop(NB, point_back)
    edge_send(2, r.hid[T : T + 16], r.hid[16:32])
    turn()

    def grad_point(k):
        cols = rows_of(k, GC)
        r.w[POINT][cols] = mm_tn(r.sep[:, cols], r.a4[...]).astype(BF16)

    loop(FF // GC, grad_point)
    reduce_start(U_POINT0, U_POINT1)
    turn()
    r.hid[0:16], r.hid[T + 16 : T + 32] = edge_take(2)

    def depth_back(j):
        cols = pl.ds(pl.multiple_of(j * 256, 256), 256)
        gain, shift = r.midp[0:1, cols], r.midp[1:2, cols]
        sums = [jnp.zeros((8, 256), F32) for _ in range(9)]
        for b in range(T // MB):
            lo = b * MB
            taps = mm(r.ms[b], r.hid[window(b) : window(b) + MW, cols])
            a3 = r.nm[lo : lo + MB, cols].astype(F32) * gain + shift
            total = jnp.zeros((MB, 256), F32)
            for o in range(9):
                moved = taps[(8 - o) * MB : (9 - o) * MB]
                total = total + moved * r.midp[2 + o : 3 + o, cols]
                part = moved * a3
                for g in range(MB // 8):
                    sums[o] = sums[o] + part[g * 8 : (g + 1) * 8]
            r.big[lo + 8 : lo + 8 + MB, cols] = total
        for o in range(9):
            r.g8[2 + o : 3 + o, cols] = jnp.sum(sums[o], axis=0, keepdims=True)

    loop(FF // 256, depth_back, turns_of(FF // 256))

    def mid_back(i):
        rows, erows = rows_of(i, RM), rows_of(i, RM, 8)
        e = r.big[erows]
        unit = r.nm[rows].astype(F32)
        eg = e * r.midp[0:1]
        m1 = jnp.mean(eg, axis=-1, keepdims=True)
        m2 = jnp.mean(eg * unit, axis=-1, keepdims=True)
        r.g8[0:1] += jnp.sum(e * unit, axis=0, keepdims=True)
        r.g8[1:2] += jnp.sum(e, axis=0, keepdims=True)
        dmid = r.rm[rows] * (eg - m1 - unit * m2)
        r.dgl[rows] = (dmid * r.dgl[rows].astype(F32)).astype(BF16)
        right = dmid[:, 0:H] * r.dgr[rows].astype(F32)
        r.pext[0, erows] = right.astype(BF16).astype(F32)

    loop(T // RM, mid_back, turns_of(T // RM))
    edge_send(3, r.pext[0, T : T + 8], r.pext[0, 8:16])
    r.tr[...] = r.a2[...].T

    def grad_left(k):
        cols = rows_of(k, GC)
        r.sep[:, cols] = mm(r.tr[...], r.dgl[:, cols]).astype(BF16)

    half = FF // GC // 2
    lax.fori_loop(0, half, lambda k, _: (grad_left(k), 0)[1], 0)
    reduce_start(U_LEFT0)
    turn()
    lax.fori_loop(half, 2 * half, lambda k, _: (grad_left(k), 0)[1], 0)
    reduce_start(U_LEFT1)
    turn()
    top, bottom = edge_take(3)
    r.pext[0, 0:8] = top
    r.pext[0, T + 8 : T + 16] = bottom
    for k in range(T // 128):
        lo = k * 128
        for o in (-1, 0, 1):
            moved = r.pext[0, lo + 8 - o : lo + 136 - o]
            if o:
                moved = moved * jnp.concatenate([mask(-o, lo, 128)] * (H // 128), axis=1)
            r.hid[lo : lo + 128, (o + 1) * H : (o + 2) * H] = moved.astype(BF16)
    for o in range(3):
        cols = slice(o * H, (o + 1) * H)
        r.dkvr[:, cols] = mm(r.tr[...], r.hid[0:T, cols]).astype(BF16)
    reduce_start(U_CONV)
    turn()

    def branch_back(i):
        rows = rows_of(i)
        e = mm_t(r.dgl[rows], r.w[LEFT][...])
        for o in range(3):
            e = e + mm_t(r.hid[rows, o * H : (o + 1) * H], r.w[CONV][o])
        r.gs[rows] += ln_back(1, e, r.y1[rows])

    loop(NB, branch_back, turns_of(NB))

    def gate_back(i):
        rows = rows_of(i)
        g = r.gs[rows]
        r.sg[rows, 0:D] = (g * r.sg[rows, 0:D].astype(F32)).astype(BF16)
        r.sg[rows, D : 2 * D] = (g * r.sg[rows, D : 2 * D].astype(F32)).astype(BF16)

    loop(NB, gate_back)
    r.tr[...] = r.a1[...].T

    def grad_glu(k):
        cols = rows_of(k, D)
        to = pl.ds(pl.multiple_of(k * D + 2 * D, D), D)
        r.hid[0:T, to] = mm(r.tr[...], r.sg[:, cols]).astype(BF16)

    grad_glu(0)
    reduce_start(U_GLU0)
    turn()
    grad_glu(1)
    reduce_start(U_GLU1)
    turn()

    def glu_back(i):
        rows = rows_of(i)
        e = mm_t(r.sg[rows], r.w[GLU][...])
        total = r.gs[rows] + ln_back(0, e, r.xin[rows].astype(F32))
        r.a5[rows] = total.astype(BF16)

    loop(NB, glu_back, turns_of(NB))
    r.gsm[0:16] = r.g8[:, 0 : FF // 2].astype(BF16)
    r.gsm[16:32] = r.g8[:, FF // 2 : FF].astype(BF16)
    reduce_start(SMALL)
    move(TAIL[0])
    tokens_out(r.a5, r.o_ig, 3)
    move(TAIL[1])
    while any(ahead.values()):
        move(range(UNITS))

    for u in range(UNITS):
        red_end(u)
    tokens_out_done(r.osend, r.o_out, 2)
    tokens_out_done(r.a5, r.o_ig, 3)
    tokens_in_sent(r.x, r.xin, 0)
    tokens_in_sent(r.ct, r.cot, 1)
    seg_sent()
    for t in range(1, n):
        small_copy(t).wait_send()


def local(
    inputs,
    segment_ids,
    cotangent,
    norm_gain,
    norm_bias,
    glu_weight,
    left_weight,
    conv_weight,
    mid_gain,
    mid_bias,
    depth_weight,
    point_weight,
    qkv_weight,
    out_weight,
    ffn_in,
    ffn_out,
):
    seqs, span, width = inputs.shape
    n = lax.axis_size("seq")
    plan = Plan(
        lax.axis_size("dp"), n, seqs, span, width, ffn_in.shape[1], conv_weight.shape[2]
    )
    q = lax.axis_index("seq")

    def placed(piece, repeats):
        if repeats == 1:
            return piece
        size = piece.shape[-1]
        tiled = jnp.tile(piece, (1,) * (piece.ndim - 1) + (repeats,))
        at = lax.broadcasted_iota(jnp.int32, tiled.shape, tiled.ndim - 1) // size
        return jnp.where(at == q % repeats, tiled, jnp.zeros_like(tiled))

    segs = placed(segment_ids.astype(F32), plan.sr)
    segs = jnp.broadcast_to(segs[:, None, :], (seqs, 8, plan.sw))
    norms = placed(jnp.concatenate([norm_gain, norm_bias], 0), plan.nr)
    norms = jnp.pad(norms, ((0, 0), (0, plan.FFn - plan.nw)))
    small = jnp.concatenate([norms, mid_gain[None], mid_bias[None], depth_weight], 0)
    small = jnp.pad(small, ((0, 32 - small.shape[0]), (0, 0)))
    weights = [None] * WEIGHTS
    weights[GLU], weights[CONV], weights[LEFT] = glu_weight, conv_weight, left_weight
    weights[POINT], weights[QKV], weights[OUT] = point_weight, qkv_weight, out_weight
    weights[FIN], weights[FOUT] = ffn_in, ffn_out

    shapes = []
    plan.buffers(shapes.append)
    out_shape = [jax.ShapeDtypeStruct(inputs.shape, BF16)] * 2
    out_shape += [jax.ShapeDtypeStruct(plan.piece(w, plan.kr(w)), BF16) for w in range(WEIGHTS)]
    out_shape += [jax.ShapeDtypeStruct((32, plan.FF // 2), BF16)]
    hbm = pl.BlockSpec(memory_space=pl.ANY)
    got = pl.pallas_call(
        lambda *refs: kernel(plan, *refs),
        out_shape=out_shape,
        in_specs=[hbm] * INPUTS,
        out_specs=[hbm] * OUTPUTS,
        scratch_shapes=shapes,
        compiler_params=pltpu.CompilerParams(
            collective_id=0, has_side_effects=True, vmem_limit_bytes=64 << 20
        ),
        name="cell",
    )(inputs, segs, cotangent, small, *weights)
    out = unpacked(plan, got)
    return (
        out[0],
        out[1],
        out[2 + WEIGHTS],
        out[3 + WEIGHTS],
        out[2 + GLU],
        out[2 + LEFT],
        out[2 + CONV],
        out[4 + WEIGHTS].reshape(-1),
        out[5 + WEIGHTS].reshape(-1),
        out[6 + WEIGHTS],
        out[2 + POINT],
        out[2 + QKV],
        out[2 + OUT],
        out[2 + FIN],
        out[2 + FOUT],
    )


def unpacked(plan, parts):
    count = 2 + WEIGHTS
    dn = plan.D // plan.n
    wide = [jax.ShapeDtypeStruct(p.shape, F32) for p in parts[:count]]
    conv, qkv, H = 2 + CONV, 2 + QKV, plan.HALF
    wide[conv] = jax.ShapeDtypeStruct((3, plan.kr(CONV), H), F32)
    tiny = [(4, dn), (4, dn), (1, plan.FFn), (1, plan.FFn), (9, plan.FFn)]
    out_shape = wide + [jax.ShapeDtypeStruct(shape, F32) for shape in tiny]

    def body(*refs):
        ins, outs = refs[:count], refs[count + 1 : 2 * count + 1]
        sums, tinies = refs[count], refs[2 * count + 1 : 2 * count + 6]
        near, far = refs[2 * count + 6 : 3 * count + 6], refs[3 * count + 6 : 4 * count + 6]
        came, went = refs[4 * count + 6], refs[4 * count + 7]

        def arrive(i):
            return pltpu.make_async_copy(ins[i], near[i], came.at[i])

        def leave(i):
            return pltpu.make_async_copy(far[i], outs[i], went.at[i])

        for i in range(count):
            arrive(i).start()
        q = lax.axis_index("seq")
        whole = jnp.concatenate([sums[0:16].astype(F32), sums[16:32].astype(F32)], axis=1)
        rolled = pltpu.roll(whole, (plan.FF - q * plan.FFn) % plan.FF, 1)[:, 0 : plan.FFn]
        tinies[2][...] = rolled[0:1]
        tinies[3][...] = rolled[1:2]
        tinies[4][...] = rolled[2:11]
        for k in range(2):
            row = whole[11 + k : 12 + k]
            rows = [row[:, i * plan.D : (i + 1) * plan.D] for i in range(4)]
            both = jnp.concatenate(rows + rows, axis=0)
            tinies[k][...] = pltpu.roll(both, (plan.D - q * dn) % plan.D, 1)[0:4, 0:dn]
        for i in range(count):
            arrive(i).wait()
            if i == conv:
                for k in range(3):
                    far[i][k] = near[i][:, k * H : (k + 1) * H].astype(F32)
            elif i == qkv:
                for k in range(12):
                    to = (k % 3) * plan.D + k // 3 * 128
                    far[i][:, to : to + 128] = near[i][:, k * 128 : (k + 1) * 128].astype(F32)
            else:
                far[i][...] = near[i][...].astype(F32)
            leave(i).start()
        for i in range(count):
            leave(i).wait()

    hbm = pl.BlockSpec(memory_space=pl.ANY)
    vmem = pl.BlockSpec(memory_space=pltpu.VMEM)
    return pl.pallas_call(
        body,
        out_shape=out_shape,
        in_specs=[hbm] * count + [vmem],
        out_specs=[hbm] * count + [vmem] * len(tiny),
        scratch_shapes=[pltpu.VMEM(p.shape, BF16) for p in parts[:count]]
        + [pltpu.VMEM(shape.shape, F32) for shape in wide]
        + [pltpu.SemaphoreType.DMA((count,))] * 2,
        compiler_params=pltpu.CompilerParams(vmem_limit_bytes=64 << 20),
    )(*parts)


def solution(mesh):
    in_specs = (
        P("dp", "seq", None),
        P("dp", "seq"),
        P("dp", "seq", None),
        P(None, "seq"),
        P(None, "seq"),
        P("seq", None),
        P("seq", None),
        P(None, "seq", None),
        P("seq"),
        P("seq"),
        P(None, "seq"),
        P("seq", None),
        P("seq", None),
        P("seq", None),
        P("seq", None),
        P("seq", None),
    )
    out_specs = (
        P("dp", "seq", None),
        P("dp", "seq", None),
        P(None, "seq"),
        P(None, "seq"),
        P("seq", None),
        P("seq", None),
        P(None, "seq", None),
        P("seq"),
        P("seq"),
        P(None, "seq"),
        P("seq", None),
        P("seq", None),
        P("seq", None),
        P("seq", None),
        P("seq", None),
    )
    return jax.shard_map(local, mesh=mesh, in_specs=in_specs, out_specs=out_specs, check_vma=False)
```

profile of v0, /device:TPU:0, one launch (start us, length us, event | category | flops | bytes accessed | tf_op | source)
XLA Modules:
  0.0 160.9 jit_solution(11743210707604873729)
XLA Ops:
  0.6 0.0 copy-start.1
  0.7 0.7 convert_element_type.7
  1.3 0.0 copy-done.1
  1.3 0.0 copy-start.2
  1.4 0.0 copy-start.3
  1.4 0.0 copy-start.4
  1.4 0.7 copy-done.2
  2.0 0.0 copy-start
  2.0 0.0 copy-done.3
  2.0 0.0 copy-done.4
  2.1 0.6 broadcast_in_dim.12.refs_1_
  2.7 0.1 copy-done
  2.7 0.6 fusion.6.refs_3_
  3.4 151.3 %cell.1 = (bf16[2,256,512]{2,1,0:T(8,128)(2,1)}, bf16[2,256,512]{2,1,0:T(8,128)(2,1)}, bf16[128,1024]{1,0:T(8,128)(2,1)}, bf16[128,768]{1,0:T(8,128)(2,1)}, bf16...) custom-call(bf16[2,256,512]{2,1,0:T(8,128)(2,1)} %refs_0_.1, ...), custom_call_target="tpu_custom_call" | custom-call | tf_op jit(solution)/shard_map/cell/pallas_call | solution.py:1484
  154.7 6.1 %shard_map.271 = (f32[2,256,512]{2,1,0:T(8,128)}, f32[2,256,512]{2,1,0:T(8,128)}, f32[128,1024]{1,0:T(8,128)}, f32[3,128,256]{2,1,0:T(8,128)}, f32[128,2048]{1,0...) custom-call(bf16[2,256,512]{2,1,0:T(8,128)(2,1)} %get-tuple-element., ...), custom_call_target="tpu_custom_call" | custom-call | tf_op jit(solution)/shard_map/pallas_call | solution.py:1566
  (3 shorter events, 0.0 us)
Async XLA Ops:
  0.6 0.7 copy-start.1
  1.3 0.7 copy-start.2
  1.4 0.7 copy-start.3
  1.4 0.7 copy-start.4
  2.0 0.7 copy-start
where the time goes:
time: 161 us
  Pallas kernels  157 us (98%)
    pallas_call x1, Pallas kernels, local(): pl.pallas_call(lambda *refs: kernel(plan, *refs), out_shape=out_shape, in...  151 us
    pallas_call x1, Pallas kernels, unpacked(): pl.pallas_call(body, out_shape=out_shape, in_specs=[hbm] * count + [vmem]...  6.07 us

commit v1 on v0

--- a/solution.py
+++ b/solution.py
@@ -20,44 +20,40 @@
 UNIT_WEIGHT = (GLU, GLU, CONV, LEFT, LEFT, POINT, POINT, QKV, QKV, OUT, FIN, FOUT, WEIGHTS)
 UNIT_PART = (0, 1, None, 0, 1, 0, 1, 0, 1, None, None, None, None)
 
-SHARED = (GLU, LEFT, POINT, FIN,)
+SHARED = (GLU, CONV, POINT,)
 SMALLS, TOKENS = 8, 9
-START = (GLU, SMALLS, LEFT, TOKENS)
+START = (GLU, CONV, SMALLS, TOKENS)
 FORWARD = (
-    ((1, GLU),),
-    (),
-    (),
-    ((1, LEFT), (2, GLU), (0, CONV), (2, LEFT), (0, POINT), (1, CONV), (0, QKV), (3, GLU)),
-    (),
-    ((1, POINT),),
-    (),
-    ((2, CONV), (3, LEFT), (0, OUT)),
+    ((1, GLU), (1, CONV)),
+    (),
+    ((0, LEFT),),
+    ((2, GLU), (2, CONV), (0, POINT), (1, LEFT), (3, GLU)),
+    (),
+    ((1, POINT), (3, CONV)),
+    ((0, QKV),),
+    (),
+    (),
+    (),
+    ((2, LEFT),),
+    ((2, POINT), (0, OUT), (0, FIN)),
+    (),
     ((1, QKV),),
     (),
-    (),
-    (),
-    ((0, FIN),),
-    ((1, OUT), (2, POINT)),
-    (),
-    ((0, FOUT),),
-    ((2, QKV),),
+    ((1, OUT),),
+    (),
+    (),
+    ((3, POINT), (0, FOUT)),
     ((1, FIN),),
     (),
     (),
-    ((2, OUT),),
-    (),
-    ((3, POINT),),
+    (),
+    ((2, QKV), (2, OUT)),
+    (),
+    (),
+    ((1, FOUT),),
     ((0, TOKENS),),
-    (),
-    (),
-    ((1, FOUT),),
-    (),
     ((2, FIN),),
-    (),
-    (),
-    (),
-    ((2, FOUT), (3, FIN)),
-    (),
+    ((2, FOUT),),
     (),
     (),
     (),
@@ -70,41 +66,46 @@
     (),
     (),
     (),
-    (U_FOUT, U_FIN, U_OUT),
-    (),
     (U_FOUT,),
-    (),
     (U_FIN,),
-    (U_FOUT, U_OUT, U_QKV0, U_QKV1),
+    (),
+    (),
+    (U_OUT,),
+    (U_FOUT,),
+    (),
+    (U_FIN, U_QKV0),
+    (U_OUT,),
+    (U_FOUT, U_QKV1),
+    (U_QKV0,),
     (),
     (U_FIN,),
-    (U_OUT, U_POINT0),
-    (U_QKV0, U_POINT1),
-    (),
-    (U_QKV1, U_FOUT),
-    (),
-    (),
-    (U_QKV0,),
-    (U_POINT0,),
-    (U_QKV1,),
-    (U_FIN,),
-    (),
-    (U_OUT, U_POINT1),
-    (U_FOUT, U_POINT0),
-    (U_QKV0,),
-    (U_LEFT0, U_LEFT1, U_QKV1),
-    (U_POINT1, U_CONV),
+    (U_POINT0, U_POINT1),
+    (U_QKV0, U_QKV1),
+    (U_FOUT,),
+    (),
+    (),
+    (),
+    (U_QKV1, U_POINT0),
+    (),
+    (),
+    (U_OUT, U_FIN),
+    (U_POINT1,),
+    (U_POINT0, U_FOUT),
+    (U_LEFT0, U_QKV1),
+    (U_QKV0, U_OUT, U_POINT1, U_LEFT1),
     (),
     (U_POINT0, U_FIN),
     (),
-    (U_OUT, U_GLU0),
+    (U_LEFT0,),
+    (U_QKV1, U_CONV, U_GLU0, U_GLU1, U_LEFT1),
 )
 TAIL = (
-    (U_GLU1, U_LEFT0, SMALL, U_QKV0, U_POINT1, U_LEFT1, U_QKV1, U_LEFT0, U_POINT0, U_CONV, U_LEFT1, U_POINT1, U_GLU0, U_LEFT0, U_GLU1, U_CONV, SMALL),
-    (U_GLU0, U_LEFT1, U_GLU1, SMALL, U_LEFT0, U_CONV, U_GLU0, U_LEFT1, U_GLU1, SMALL, U_CONV, U_GLU0, U_GLU1, SMALL, U_FOUT, U_FIN, U_OUT, U_QKV0, U_QKV1, U_POINT0, U_POINT1, U_LEFT0, U_LEFT1, U_CONV, U_GLU0, U_GLU1, SMALL),
+    (SMALL, U_POINT1, U_QKV0, U_LEFT0, U_OUT, U_CONV, U_POINT0, U_LEFT1, U_GLU0, U_LEFT0, U_POINT1, U_GLU1, SMALL),
+    (U_CONV, U_GLU0, U_LEFT1, U_GLU1, U_LEFT0, SMALL, U_CONV, U_GLU0, U_LEFT1, U_GLU1, SMALL, U_CONV, U_GLU0, U_GLU1, SMALL, U_FOUT, U_FIN, U_OUT, U_QKV0, U_QKV1, U_POINT0, U_POINT1, U_LEFT0, U_LEFT1, U_CONV, U_GLU0, U_GLU1, SMALL),
 )
 
 MB, MW = 128, 256
+TAPS = (-4, -3, -2, -1, 1, 2, 3, 4)
 FAR = -(2.0**30)
 
 
@@ -162,6 +163,8 @@
         self.nw = max(dn, 128)
         self.nr = self.nw // dn
         self.FFn = hidden // n
+        self.srows = 8 * self.nw // self.FFn
+        self.spack = -(-(self.srows + 11) // 16) * 16
         self.dims = [
             (width, 2 * width),
             (width, half),
@@ -212,15 +215,15 @@
         if self.Z > 1:
             r.u = [vm(shape, dtype) for shape, dtype in parts]
             r.d = [vm(shape, dtype) for shape, dtype in parts]
-        r.segbuf = vm((n, 8, self.sw), F32)
+        r.segbuf = vm((n, 8, self.sw), jnp.int32)
         r.segrow = vm((8, self.LEN), F32)
         r.segcol = vm((self.LEN + 16, 128), F32)
         r.segloc = vm((T + 16, 128), F32)
         r.mext = vm((T + 16, 128), F32)
-        r.ms = vm((T // MB, 9 * MB, MW), BF16)
+        r.ms = vm((T // MB, 8 * MB, MW), BF16)
         r.qenc = vm((T, 128), BF16)
         r.kenc = vm((self.LEN, 128), BF16)
-        r.smallbuf = vm((n, 32, self.FFn), BF16)
+        r.smallbuf = vm((n, self.spack, self.FFn), BF16)
         r.nrm = vm((8, D), F32)
         r.midp = vm((16, FF), F32)
         r.xin = vm((T, D), BF16)
@@ -257,21 +260,18 @@
         r.s_as = sem(WEIGHTS)
         r.s_ar = sem(WEIGHTS, self.B - 1)
         r.s_br = sem(WEIGHTS, (self.A - 1) * self.B)
-        r.s_ds = sem(WEIGHTS)
         r.s_dr = sem(WEIGHTS)
         if self.shared:
-            r.s_hs = sem(WEIGHTS)
             r.s_hr = sem(WEIGHTS)
         r.s_rs = sem(UNITS)
         r.s_rr = sem(UNITS)
-        r.s_ps = sem(UNITS, 2)
+        r.s_ps = sem(UNITS)
         r.s_pr = sem(UNITS, 2)
         if self.Z > 1:
-            r.s_zs = sem(UNITS, 2)
+            r.s_zs = sem(UNITS)
             r.s_zr = sem(UNITS, 2)
         r.s_fs = sem(UNITS)
         r.s_fr = sem(UNITS)
-        r.s_fl = sem(UNITS)
         r.s_xs = sem(4, self.S)
         r.s_xr = sem(4, max(self.PH, self.S))
         r.s_gs = sem(2 * self.S)
@@ -280,8 +280,8 @@
         r.s_mr = sem(n)
         r.s_es = sem(4)
         r.s_er = sem(4)
-        r.s_ks = sem(1)
-        r.s_kr = sem(1)
+        r.s_ks = sem(HEADS // 2)
+        r.s_kr = sem(HEADS // 2)
         r.s_js = sem(HEADS // 2)
         r.s_jr = sem(HEADS // 2)
         return r
@@ -387,9 +387,9 @@
 
     def pass_on(w, u, t):
         blk = wblock(w, shard_from(u, t))
-        remote(blk, blk, r.s_ds.at[w], r.s_dr.at[w], sibling).start()
+        remote(blk, blk, r.s_as.at[w], r.s_dr.at[w], sibling).start()
         if w in plan.shared:
-            remote(blk, blk, r.s_hs.at[w], r.s_hr.at[w], partner).start()
+            remote(blk, blk, r.s_as.at[w], r.s_hr.at[w], partner).start()
 
     def local_shard(w):
         dst = vrows(r.w[w], w, q * plan.kr(w), plan.kr(w))
@@ -426,7 +426,7 @@
             for t in range(B):
                 if (u, t) != (0, 0):
                     blk = wblock(w, shard_from(u, t), 1 - par)
-                    remote(blk, blk, r.s_ds.at[w], r.s_dr.at[w], sibling).start()
+                    remote(blk, blk, r.s_as.at[w], r.s_dr.at[w], sibling).start()
 
     def g3(w):
         local_shard(w).wait()
@@ -450,10 +450,7 @@
         return [(k, lambda steps=steps: gather(steps)) for k, steps in every if steps]
 
     def gather_sent(w):
-        bytes_of(others(w), r.s_as.at[w]).wait()
-        bytes_of(vrows(r.w[w], w, 0, (n - 1) * plan.hr(w)), r.s_ds.at[w]).wait()
-        if w in plan.shared:
-            bytes_of(others(w), r.s_hs.at[w]).wait()
+        bytes_of(vrows(r.w[w], w, 0, 2 * (n - 1) * plan.hr(w)), r.s_as.at[w]).wait()
 
     def token_rows(ref, slot):
         return ref.at[pl.ds(aligned(slot * span), span)]
@@ -653,12 +650,23 @@
         for s in range(shards(u)):
             copy_r(u, s).start()
 
-    def plus(a, b):
-        return a[...].astype(F32) + b[...].astype(F32)
+    def put(to, *terms):
+        size = to.shape[0]
+        rows = min(size, 32)
+
+        def some(i, _):
+            at = pl.ds(pl.multiple_of(i * rows, rows), rows)
+            total = terms[0][at].astype(F32)
+            for term in terms[1:]:
+                total = total + term[at].astype(F32)
+            to[at] = total.astype(to.dtype)
+            return 0
+
+        lax.fori_loop(0, size // rows, some, 0)
 
     def add_core(u, s):
         mine = gpiece(u, s, c)
-        mine[...] = plus(mine, rpiece(u, s)).astype(mine.dtype)
+        put(mine, mine, rpiece(u, s))
 
     def slot1(u, t):
         return (u - 1) * B + t
@@ -670,7 +678,7 @@
         return remote(
             gpiece(u, qof(c, f_ + t, g_ + k), c),
             ppiece(u, slot1(k, t)),
-            r.s_ps.at[u, 0],
+            r.s_ps.at[u],
             r.s_pr.at[u, 0],
             dev(c, qof(c, f_, g_ + k)),
         )
@@ -680,7 +688,7 @@
         return remote(
             r.r[WEIGHTS] if u == SMALL else gpiece(u, to, c),
             ppiece(u, slot2(t)),
-            r.s_ps.at[u, 1],
+            r.s_ps.at[u],
             r.s_pr.at[u, 1],
             dev(c, to),
         )
@@ -710,14 +718,9 @@
         all_p(u, 0, r.s_pr).wait()
 
         def send(t, _):
-            if u == SMALL:
-                total, to = gpiece(u, 0, c)[...].astype(F32), r.r[WEIGHTS]
-            else:
-                to = gpiece(u, qof(c, f_ + t, g_), c)
-                total = to[...].astype(F32)
-            for k in range(1, A):
-                total = total + ppiece(u, slot1(k, 0 if u == SMALL else t))[...].astype(F32)
-            to[...] = total.astype(to.dtype)
+            mine = gpiece(u, 0 if u == SMALL else qof(c, f_ + t, g_), c)
+            came = [ppiece(u, slot1(k, 0 if u == SMALL else t)) for k in range(1, A)]
+            put(r.r[WEIGHTS] if u == SMALL else mine, mine, *came)
             if u != SMALL:
                 copy_p2(u, t).start()
             return 0
@@ -731,20 +734,15 @@
 
     def red2(u):
         all_p(u, 1, r.s_pr).wait()
-        total = (r.r[WEIGHTS] if u == SMALL else gpiece(u, q, c))[...].astype(F32)
-        if u != SMALL:
-            for k in range(1, A):
-                total = total + ppiece(u, slot1(k, 0))[...].astype(F32)
-        for t in range(1, B):
-            total = total + ppiece(u, slot2(t))[...].astype(F32)
-        mine = ppiece(u, 0)
-        mine[...] = total.astype(mine.dtype)
+        came = [] if u == SMALL else [ppiece(u, slot1(k, 0)) for k in range(1, A)]
+        came += [ppiece(u, slot2(t)) for t in range(1, B)]
+        put(ppiece(u, 0), r.r[WEIGHTS] if u == SMALL else gpiece(u, q, c), *came)
 
     def copy_z(u, way):
         return remote(
             ppiece(u, 1 + way),
             zpiece(u, way),
-            r.s_zs.at[u, way],
+            r.s_zs.at[u],
             r.s_zr.at[u, way],
             dev(c, q, z + 1 if way == 0 else z - 1),
         )
@@ -755,21 +753,21 @@
         @pl.when(z == h)
         def _():
             if h == 0:
-                up[...] = own[...]
+                put(up, own)
             else:
                 copy_z(u, 0).wait_recv()
-                up[...] = plus(own, zpiece(u, 0)).astype(up.dtype)
+                put(up, own, zpiece(u, 0))
             if h < Z - 1:
                 copy_z(u, 0).start()
 
         @pl.when(z == Z - 1 - h)
         def _():
             if h == 0:
-                down[...] = own[...]
+                put(down, own)
             else:
                 copy_z(u, 1).wait_recv()
                 if h < Z - 1:
-                    down[...] = plus(own, zpiece(u, 1)).astype(down.dtype)
+                    put(down, own, zpiece(u, 1))
             if h < Z - 1:
                 copy_z(u, 1).start()
 
@@ -780,7 +778,7 @@
         return urows(r.o[w], u, c * plan.hr(w), plan.hr(w))
 
     def final_local(u):
-        return pltpu.make_async_copy(ppiece(u, 0), final_rows(u), r.s_fl.at[u])
+        return pltpu.make_async_copy(ppiece(u, 0), final_rows(u), r.s_fs.at[u])
 
     def final_remote(u):
         return remote(ppiece(u, 0), final_rows(u), r.s_fs.at[u], r.s_fr.at[u], sibling)
@@ -791,30 +789,30 @@
 
             @pl.when(z == Z - 1)
             def _():
-                own[...] = up[...]
+                put(own, up)
 
             @pl.when(z < Z - 1)
             def _():
-                own[...] = plus(up, zpiece(u, 1)).astype(own.dtype)
+                put(own, up, zpiece(u, 1))
 
         final_local(u).start()
         final_remote(u).start()
 
     def red_end(u):
-        final_local(u).wait()
-        final_remote(u).wait()
+        final_remote(u).wait_recv()
+        bytes_of(slots(u, 0, 2), r.s_fs.at[u]).wait()
         all_r(u, r.s_rs).wait()
-        all_p(u, 0, r.s_ps).wait()
-        all_p(u, 1, r.s_ps).wait()
+        bytes_of(slots(u, 0, A + B - 2 if u == SMALL else n - 1), r.s_ps.at[u]).wait()
         if Z > 1:
-
-            @pl.when(z < Z - 1)
+            ends = jnp.logical_or(z == 0, z == Z - 1)
+
+            @pl.when(ends)
             def _():
-                copy_z(u, 0).wait_send()
-
-            @pl.when(z > 0)
+                bytes_of(slots(u, 0, 1), r.s_zs.at[u]).wait()
+
+            @pl.when(jnp.logical_not(ends))
             def _():
-                copy_z(u, 1).wait_send()
+                bytes_of(slots(u, 0, 2), r.s_zs.at[u]).wait()
 
     def red2_hop(u):
         red2(u)
@@ -894,7 +892,7 @@
         got = r.segbuf[grp * plan.sr]
         for k in range(1, plan.sr):
             got = got + r.segbuf[grp * plan.sr + k]
-        r.segrow[:, grp * plan.sw : (grp + 1) * plan.sw] = got
+        r.segrow[:, grp * plan.sw : (grp + 1) * plan.sw] = got.astype(F32)
     r.segcol[0:8] = jnp.full((8, 128), -1.0, F32)
     r.segcol[plan.LEN + 8 : plan.LEN + 16] = jnp.full((8, 128), -1.0, F32)
     for k in range(plan.LEN // 128):
@@ -911,12 +909,17 @@
     for t in range(1, n):
         small_arrived(t).wait_recv()
     for grp in range(n // plan.nr):
-        got = r.smallbuf[grp * plan.nr].astype(F32)[0:8, 0 : plan.nw]
+        got = r.smallbuf[grp * plan.nr].astype(F32)
         for k in range(1, plan.nr):
-            got = got + r.smallbuf[grp * plan.nr + k].astype(F32)[0:8, 0 : plan.nw]
-        r.nrm[:, grp * plan.nw : (grp + 1) * plan.nw] = got
+            got = got + r.smallbuf[grp * plan.nr + k].astype(F32)
+        for k in range(8):
+            row, first = divmod(k * plan.nw, plan.FFn)
+            r.nrm[k : k + 1, grp * plan.nw : (grp + 1) * plan.nw] = got[
+                row : row + 1, first : first + plan.nw
+            ]
     for s in range(n):
-        r.midp[:, s * plan.FFn : (s + 1) * plan.FFn] = r.smallbuf[s].astype(F32)[8:24]
+        rows = r.smallbuf[s].astype(F32)[plan.srows : plan.srows + 11]
+        r.midp[0:11, s * plan.FFn : (s + 1) * plan.FFn] = rows
 
     def ln_out(k, v):
         unit, _ = normed(v)
@@ -942,12 +945,12 @@
     )
     for b in range(T // MB):
         home = r.segloc[8 + b * MB : 8 + (b + 1) * MB]
-        for o in range(-4, 5):
+        for i, o in enumerate(TAPS):
             there = r.segloc[8 + b * MB + o : 8 + (b + 1) * MB + o]
             same = jnp.where(home == there, 1.0, 0.0)
             hit = ahead_of == b * MB + 16 - window(b) + o
             tap = jnp.where(hit, jnp.concatenate([same] * (MW // 128), axis=1), 0.0)
-            r.ms[b, (o + 4) * MB : (o + 5) * MB] = tap.astype(BF16)
+            r.ms[b, i * MB : (i + 1) * MB] = tap.astype(BF16)
 
     lane = lax.broadcasted_iota(jnp.int32, (1, 128), 1)
     lane_f = lane.astype(F32)
@@ -1031,58 +1034,65 @@
     pass_turn()
 
     def depthwise(j):
-        cols = pl.ds(pl.multiple_of(j * 256, 256), 256)
+        cols = pl.ds(pl.multiple_of(j * 512, 512), 512)
         for b in range(T // MB):
             near = r.hid[window(b) : window(b) + MW, cols]
             taps = mm(r.ms[b], near)
-            total = taps[0:MB] * r.midp[2:3, cols]
-            for o in range(1, 9):
-                total = total + taps[o * MB : (o + 1) * MB] * r.midp[2 + o : 3 + o, cols]
+            total = r.hid[16 + b * MB : 16 + (b + 1) * MB, cols].astype(F32) * r.midp[6:7, cols]
+            for i, o in enumerate(TAPS):
+                total = total + taps[i * MB : (i + 1) * MB] * r.midp[6 + o : 7 + o, cols]
             r.sep[b * MB : (b + 1) * MB, cols] = total.astype(BF16)
 
-    loop(FF // 256, depthwise, pass_turns(FF // 256))
+    loop(FF // 512, depthwise, pass_turns(FF // 512))
     pass_turn()
     g3(POINT)
 
     def point(i):
-        rows = rows_of(i)
+        rows = rows_of(i, T)
         y2 = r.y1[rows] + mm(r.sep[rows], r.w[POINT][...])
         r.y2[rows] = y2
         r.a4[rows] = ln_out(2, y2)
 
-    loop(NB, point)
+    loop(1, point)
     pass_turn()
     pass_turn()
     g3(QKV)
     scale = 1.0 / math.sqrt(D // HEADS)
 
-    def qkv(i):
+    def keys_values(i):
         rows = rows_of(i)
         a4 = r.a4[rows]
-        r.qb[rows] = (mm(a4, r.w[QKV][:, 0:D]) * scale).astype(BF16)
         here = pl.ds(pl.multiple_of(c * T + i * RB, RB), RB)
         r.kvb[here, 0:D] = mm(a4, r.w[QKV][:, D : 2 * D]).astype(BF16)
         r.kvb[here, D : 2 * D] = mm(a4, r.w[QKV][:, 2 * D : 3 * D]).astype(BF16)
 
-    loop(NB, qkv)
-
-    def kv_copy():
-        blk = r.kvb.at[pl.ds(aligned(c * T), T)]
-        return remote(blk, blk, r.s_ks.at[0], r.s_kr.at[0], sibling)
-
-    kv_copy().start()
-    pass_turn()
-    heads_lanes = [lane < 64, lane >= 64]
-    kv_copy().wait()
-    pass_turn()
+    def queries(i):
+        rows = rows_of(i)
+        r.qb[rows] = (mm(r.a4[rows], r.w[QKV][:, 0:D]) * scale).astype(BF16)
+
+    def kv_copy(j, base):
+        blk = r.kvb.at[pl.ds(aligned(c * T), T), pair_cols(j, base)]
+        return remote(blk, blk, r.s_ks.at[j], r.s_kr.at[j], sibling)
 
     def pair_cols(j, base=0):
         return pl.ds(pl.multiple_of(j * 128 + base, 128), 128)
 
+    def pair_bytes(j, semaphore):
+        return bytes_of(r.kvb.at[pl.ds(0, T), pl.ds(0, 256)], semaphore.at[j])
+
+    loop(NB, keys_values)
+    for j in range(HEADS // 2):
+        kv_copy(j, 0).start()
+        kv_copy(j, D).start()
+    loop(NB, queries)
+    pass_turn()
+    pass_turn()
+    heads_lanes = [lane < 64, lane >= 64]
     def head_lanes(e, v):
         return jnp.where(heads_lanes[e], v, jnp.zeros_like(v))
 
     def attend(j):
+        pair_bytes(j, r.s_kr).wait()
         cols, vcols = pair_cols(j), pair_cols(j, D)
         keys = jnp.concatenate([r.kvb[:, cols], r.kenc[...]], axis=1)
         for k in range(T // RB):
@@ -1106,12 +1116,12 @@
     g3(OUT)
 
     def out(i):
-        rows = rows_of(i)
+        rows = rows_of(i, T)
         y3 = r.y2[rows] + mm(r.ctx[rows], r.w[OUT][...])
         r.y3[rows] = y3
         r.a5[rows] = ln_out(3, y3)
 
-    loop(NB, out)
+    loop(1, out)
     pass_turn()
     pass_turn()
     g3(FIN)
@@ -1129,19 +1139,21 @@
     g3(FOUT)
 
     def ffn_out(i):
-        rows = rows_of(i)
+        rows = rows_of(i, T)
         r.osend[rows] = (r.y3[rows] + mm(r.hid[rows], r.w[FOUT][...])).astype(BF16)
 
-    loop(NB, ffn_out)
+    loop(1, ffn_out)
     pass_turn()
     tokens_out(r.osend, r.o_out, 2)
     for w in range(WEIGHTS):
         gather_sent(w)
+    for j in range(HEADS // 2):
+        pair_bytes(j, r.s_ks).wait()
 
     tokens_in_done(r.cot, 1)
 
     def ffn_back(i):
-        rows = rows_of(i)
+        rows = rows_of(i, T)
         f4 = r.cot[rows]
         for k in range(FF // CH):
             cols = slice(k * CH, (k + 1) * CH)
@@ -1150,7 +1162,7 @@
         e = mm_t(r.dg[rows], r.w[FIN][...])
         r.gs[rows] = f4.astype(F32) + ln_back(3, e, r.y3[rows])
 
-    loop(NB, ffn_back)
+    loop(1, ffn_back)
     GC = 1024
 
     def grad_outer(k):
@@ -1171,12 +1183,12 @@
     turn()
 
     def out_back(i):
-        rows = rows_of(i)
+        rows = rows_of(i, T)
         f3 = r.gs[rows].astype(BF16)
         r.a5[rows] = f3
         r.hid[rows, 3 * D : 4 * D] = mm_t(f3, r.w[OUT][...]).astype(BF16)
 
-    loop(NB, out_back)
+    loop(1, out_back)
     r.w[OUT][...] = mm_tn(r.ctx[...], r.a5[...]).astype(BF16)
     reduce_start(U_OUT)
     turn()
@@ -1191,17 +1203,20 @@
         terms = jnp.where(lane == 4, high, jnp.where(lane == 5, mid, jnp.where(lane == 6, low, 0.0)))
         return extra - terms.astype(BF16)
 
+    halfway = []
+
     def attend_back(j):
         cols, vcols = pair_cols(j), pair_cols(j, D)
         k2 = r.kvb[:, cols]
         keys = jnp.concatenate([k2, r.kenc[...]], axis=1)
+        turned = [head_lanes(e, k2).T for e in range(2)]
         values = jnp.concatenate([r.kvb[:, vcols], r.kenc[...]], axis=1)
         for k in range(T // QB):
             rows = slice(k * QB, (k + 1) * QB)
             q2 = r.qb[rows, cols]
             d2 = r.hid[rows, pair_cols(j, 3 * D)]
             inner = d2.astype(F32) * r.ctx[rows, cols].astype(F32)
-            dq = jnp.zeros((QB, 128), F32)
+            dq = jnp.zeros((128, QB), F32)
             for e in range(2):
                 qe, de = head_lanes(e, q2), head_lanes(e, d2)
                 lse = jnp.sum(
@@ -1224,12 +1239,19 @@
                     else:
                         r.big[0:T, at : at + 128] += dk[half]
                         r.big[0:T, at + 256 : at + 384] += dv[half]
-                dq = dq + mm_tn(ds, head_lanes(e, k2))
-            r.hid[rows, cols] = (dq * scale).astype(BF16)
+                dq = dq + mm(turned[e], ds)
+            r.hid[rows, cols] = (dq.T * scale).astype(BF16)
+            if k == 0:
+                for step, act in halfway:
+                    pl.when(j == step)(lambda act=act: (act(), None)[1])
 
         def part(core, what):
             at = pl.multiple_of(2 * D + core * 128 + what * 256, 128)
             return r.big[0:T, pl.ds(at, 128)]
+
+        @pl.when(j >= 2)
+        def _():
+            dkv_copy(j - 2).wait_send()
 
         for what in range(2):
             mine = pl.ds(pl.multiple_of(j * 256 + what * 128, 128), 128)
@@ -1239,9 +1261,9 @@
             ).astype(BF16)
         dkv_copy(j).start()
 
-        @pl.when(j > 0)
+        @pl.when(j == 2)
         def _():
-            pair_back(j - 1)
+            pairs_back(0)
 
     def dkv_copy(j):
         slot = lax.rem(j, 2)
@@ -1253,30 +1275,35 @@
             sibling,
         )
 
-    def pair_back(j):
-        dkv_copy(j).wait()
-        both = pl.ds(pl.multiple_of(j * 256, 256), 256)
-        dkv = (r.big[0:T, both] + r.dkvr[:, both].astype(F32)).astype(BF16)
-        pair = jnp.concatenate([r.hid[0:T, pair_cols(j)], dkv], axis=1)
-        weight = jnp.concatenate([r.w[QKV][:, pair_cols(j, base)] for base in (0, D, 2 * D)], axis=1)
-        share = mm_t(pair, weight)
-
-        @pl.when(j == 0)
-        def _():
+    def pairs_back(m):
+        parts, weights = [], []
+        for j in (2 * m, 2 * m + 1):
+            dkv_copy(j).wait_recv()
+            if m == 1:
+                dkv_copy(j).wait_send()
+            both = slice(j * 256, (j + 1) * 256)
+            dkv = r.big[0:T, both] + r.dkvr[:, both].astype(F32)
+            own = slice(j * 128, (j + 1) * 128)
+            parts += [r.hid[0:T, own], dkv.astype(BF16)]
+            for base in (0, D, 2 * D):
+                weights.append(r.w[QKV][:, base + j * 128 : base + (j + 1) * 128])
+        pairs = jnp.concatenate(parts, axis=1)
+        share = mm_t(pairs, jnp.concatenate(weights, axis=1))
+        if m == 0:
             r.big[0:T, 3 * D : 4 * D] = share
-
-        @pl.when(j > 0)
-        def _():
+        else:
             r.big[0:T, 3 * D : 4 * D] += share
-
-        grad = mm(r.tr[...], pair)
-        r.dg[:, pl.ds(pl.multiple_of(j * 384, 128), 384)] = grad.astype(BF16)
-
-    acts = turns_of(3)
-    enlist(U_QKV0)
-    acts += [(2, lambda: red0(U_QKV0))] + [(k + 3, act) for k, act in turns_of(1)]
+        r.dg[:, m * 768 : (m + 1) * 768] = mm(r.tr[...], pairs).astype(BF16)
+
+    acts = []
+    for k in range(HEADS // 2):
+        halfway += [(k, act) for _, act in turns_of(1)]
+        if k == 2:
+            enlist(U_QKV0)
+            acts.append((2, lambda: red0(U_QKV0)))
+        acts += [(k, act) for _, act in turns_of(1)]
     loop(HEADS // 2, attend_back, acts)
-    pair_back(HEADS // 2 - 1)
+    pairs_back(1)
     reduce_start(U_QKV1)
     turn()
 
@@ -1287,15 +1314,15 @@
     loop(NB, qkv_back)
 
     def point_back(i):
-        rows = rows_of(i)
+        rows = rows_of(i, T)
         f2 = r.gs[rows].astype(BF16)
         r.a4[rows] = f2
         for k in range(FF // CH):
             cols = slice(k * CH, (k + 1) * CH)
             d = mm_t(f2, r.w[POINT][cols])
-            r.hid[rows_of(i, RB, 16), cols] = d.astype(BF16)
-
-    loop(NB, point_back)
+            r.hid[rows_of(i, T, 16), cols] = d.astype(BF16)
+
+    loop(1, point_back)
     edge_send(2, r.hid[T : T + 16], r.hid[16:32])
     turn()
 
@@ -1317,12 +1344,14 @@
             taps = mm(r.ms[b], r.hid[window(b) : window(b) + MW, cols])
             a3 = r.nm[lo : lo + MB, cols].astype(F32) * gain + shift
             total = jnp.zeros((MB, 256), F32)
-            for o in range(9):
-                moved = taps[(8 - o) * MB : (9 - o) * MB]
-                total = total + moved * r.midp[2 + o : 3 + o, cols]
+            here = r.hid[16 + lo : 16 + lo + MB, cols].astype(F32)
+            for o in range(-4, 5):
+                i = TAPS.index(-o) if o else 0
+                moved = taps[i * MB : (i + 1) * MB] if o else here
+                total = total + moved * r.midp[6 + o : 7 + o, cols]
                 part = moved * a3
                 for g in range(MB // 8):
-                    sums[o] = sums[o] + part[g * 8 : (g + 1) * 8]
+                    sums[o + 4] = sums[o + 4] + part[g * 8 : (g + 1) * 8]
             r.big[lo + 8 : lo + 8 + MB, cols] = total
         for o in range(9):
             r.g8[2 + o : 3 + o, cols] = jnp.sum(sums[o], axis=0, keepdims=True)
@@ -1464,12 +1493,12 @@
         at = lax.broadcasted_iota(jnp.int32, tiled.shape, tiled.ndim - 1) // size
         return jnp.where(at == q % repeats, tiled, jnp.zeros_like(tiled))
 
-    segs = placed(segment_ids.astype(F32), plan.sr)
+    segs = placed(segment_ids, plan.sr)
     segs = jnp.broadcast_to(segs[:, None, :], (seqs, 8, plan.sw))
     norms = placed(jnp.concatenate([norm_gain, norm_bias], 0), plan.nr)
-    norms = jnp.pad(norms, ((0, 0), (0, plan.FFn - plan.nw)))
+    norms = norms.reshape(plan.srows, plan.FFn)
     small = jnp.concatenate([norms, mid_gain[None], mid_bias[None], depth_weight], 0)
-    small = jnp.pad(small, ((0, 32 - small.shape[0]), (0, 0)))
+    small = jnp.pad(small, ((0, plan.spack - small.shape[0]), (0, 0)))
     weights = [None] * WEIGHTS
     weights[GLU], weights[CONV], weights[LEFT] = glu_weight, conv_weight, left_weight
     weights[POINT], weights[QKV], weights[OUT] = point_weight, qkv_weight, out_weight

time: 161 us -> 159 us (0.988)
  Pallas kernels: 157 us -> 154 us
    pallas_call x1, Pallas kernels: 151 us -> 148 us  [local(): pl.pallas_call(lambda *refs: kernel(plan, *refs), out_shape=out_shape, in...]
where the time goes in v1:
time: 159 us
  Pallas kernels  154 us (97%)
  other arithmetic  2.06 us (1%)
  local copies, waits for them, and re-layouts  1.97 us (1%)
    pallas_call x1, Pallas kernels, local(): pl.pallas_call(lambda *refs: kernel(plan, *refs), out_shape=out_shape, in...  148 us
    pallas_call x1, Pallas kernels, unpacked(): pl.pallas_call(body, out_shape=out_shape, in_specs=[hbm] * count + [vmem]...  6.07 us

profile of v1, /device:TPU:0, one launch (start us, length us, event | category | flops | bytes accessed | tf_op | source)
XLA Modules:
  0.0 159.0 jit_solution(16930760306227695249)
XLA Ops:
  0.6 0.7 pad_maximum_fusion
  1.4 0.0 copy-start.1
  1.4 0.7 copy-done.1
  2.0 0.0 copy-start.2
  2.0 0.7 copy-done.2
  2.7 0.0 copy-start
  2.7 1.4 fusion.6.refs_3_
  4.1 0.0 copy-done
  4.1 0.6 broadcast_in_dim.12.refs_1_
  4.7 148.1 %cell.1 = (bf16[2,256,512]{2,1,0:T(8,128)(2,1)}, bf16[2,256,512]{2,1,0:T(8,128)(2,1)}, bf16[128,1024]{1,0:T(8,128)(2,1)}, bf16[128,768]{1,0:T(8,128)(2,1)}, bf16...) custom-call(bf16[2,256,512]{2,1,0:T(8,128)(2,1)} %refs_0_.1, ...), custom_call_target="tpu_custom_call" | custom-call | tf_op jit(solution)/shard_map/cell/pallas_call | solution.py:1513
  152.8 6.1 %shard_map.271 = (f32[2,256,512]{2,1,0:T(8,128)}, f32[2,256,512]{2,1,0:T(8,128)}, f32[128,1024]{1,0:T(8,128)}, f32[3,128,256]{2,1,0:T(8,128)}, f32[128,2048]{1,0...) custom-call(bf16[2,256,512]{2,1,0:T(8,128)(2,1)} %get-tuple-element., ...), custom_call_target="tpu_custom_call" | custom-call | tf_op jit(solution)/shard_map/pallas_call | solution.py:1595
  (3 shorter events, 0.0 us)
Async XLA Ops:
  1.4 0.7 copy-start.1
  2.0 0.7 copy-start.2
  2.7 1.4 copy-start

commit v2 on v1

--- a/solution.py
+++ b/solution.py
@@ -27,8 +27,8 @@
     ((1, GLU), (1, CONV)),
     (),
     ((0, LEFT),),
-    ((2, GLU), (2, CONV), (0, POINT), (1, LEFT), (3, GLU)),
-    (),
+    ((2, GLU), (2, CONV), (0, POINT), (3, GLU)),
+    ((1, LEFT),),
     ((1, POINT), (3, CONV)),
     ((0, QKV),),
     (),
@@ -163,8 +163,7 @@
         self.nw = max(dn, 128)
         self.nr = self.nw // dn
         self.FFn = hidden // n
-        self.srows = 8 * self.nw // self.FFn
-        self.spack = -(-(self.srows + 11) // 16) * 16
+        self.spack = 32
         self.dims = [
             (width, 2 * width),
             (width, half),
@@ -215,7 +214,7 @@
         if self.Z > 1:
             r.u = [vm(shape, dtype) for shape, dtype in parts]
             r.d = [vm(shape, dtype) for shape, dtype in parts]
-        r.segbuf = vm((n, 8, self.sw), jnp.int32)
+        r.segbuf = vm((n, self.S, self.sw), jnp.int32)
         r.segrow = vm((8, self.LEN), F32)
         r.segcol = vm((self.LEN + 16, 128), F32)
         r.segloc = vm((T + 16, 128), F32)
@@ -536,12 +535,12 @@
 
                 @pl.when(here)
                 def _():
-                    pltpu.make_async_copy(r.seg.at[j], r.segbuf.at[q], r.s_gr.at[q]).start()
+                    pltpu.make_async_copy(r.seg, r.segbuf.at[q], r.s_gr.at[q]).start()
 
                 @pl.when(jnp.logical_not(here))
                 def _():
                     remote(
-                        r.seg.at[j],
+                        r.seg,
                         r.segbuf.at[q],
                         r.s_gs.at[i],
                         r.s_gr.at[q],
@@ -557,7 +556,7 @@
                 @pl.when(jnp.logical_not(here))
                 def _():
                     remote(
-                        r.seg.at[j],
+                        r.seg,
                         r.segbuf.at[q],
                         r.s_gs.at[2 * j + core],
                         r.s_gr.at[q],
@@ -652,7 +651,7 @@
 
     def put(to, *terms):
         size = to.shape[0]
-        rows = min(size, 32)
+        rows = min(size, 64)
 
         def some(i, _):
             at = pl.ds(pl.multiple_of(i * rows, rows), rows)
@@ -888,11 +887,13 @@
     for s in range(n):
         blk = r.segbuf.at[s]
         pltpu.make_async_copy(blk, blk, r.s_gr.at[s]).wait()
+    mine = lax.broadcasted_iota(jnp.int32, (S, plan.sw), 0) == lax.rem(q, S)
     for grp in range(n // plan.sr):
         got = r.segbuf[grp * plan.sr]
         for k in range(1, plan.sr):
             got = got + r.segbuf[grp * plan.sr + k]
-        r.segrow[:, grp * plan.sw : (grp + 1) * plan.sw] = got.astype(F32)
+        row = jnp.sum(jnp.where(mine, got.astype(F32), 0.0), axis=0, keepdims=True)
+        r.segrow[0:1, grp * plan.sw : (grp + 1) * plan.sw] = row
     r.segcol[0:8] = jnp.full((8, 128), -1.0, F32)
     r.segcol[plan.LEN + 8 : plan.LEN + 16] = jnp.full((8, 128), -1.0, F32)
     for k in range(plan.LEN // 128):
@@ -912,13 +913,9 @@
         got = r.smallbuf[grp * plan.nr].astype(F32)
         for k in range(1, plan.nr):
             got = got + r.smallbuf[grp * plan.nr + k].astype(F32)
-        for k in range(8):
-            row, first = divmod(k * plan.nw, plan.FFn)
-            r.nrm[k : k + 1, grp * plan.nw : (grp + 1) * plan.nw] = got[
-                row : row + 1, first : first + plan.nw
-            ]
+        r.nrm[:, grp * plan.nw : (grp + 1) * plan.nw] = got[0:8, 0 : plan.nw]
     for s in range(n):
-        rows = r.smallbuf[s].astype(F32)[plan.srows : plan.srows + 11]
+        rows = r.smallbuf[s].astype(F32)[8:19]
         r.midp[0:11, s * plan.FFn : (s + 1) * plan.FFn] = rows
 
     def ln_out(k, v):
@@ -943,14 +940,18 @@
     ahead_of = lax.broadcasted_iota(jnp.int32, (MB, MW), 1) - lax.broadcasted_iota(
         jnp.int32, (MB, MW), 0
     )
-    for b in range(T // MB):
-        home = r.segloc[8 + b * MB : 8 + (b + 1) * MB]
+    def shift_matrices(b):
+        near = r.segloc[pl.ds(pl.multiple_of(b * MB, MB), MB + 16)]
+        home = near[8 : MB + 8]
+        first = jnp.where(b == 0, 16, jnp.where(b == T // MB - 1, MW - MB - 16, (MW - MB) // 2))
         for i, o in enumerate(TAPS):
-            there = r.segloc[8 + b * MB + o : 8 + (b + 1) * MB + o]
-            same = jnp.where(home == there, 1.0, 0.0)
-            hit = ahead_of == b * MB + 16 - window(b) + o
-            tap = jnp.where(hit, jnp.concatenate([same] * (MW // 128), axis=1), 0.0)
+            same = jnp.where(home == near[8 + o : MB + 8 + o], 1.0, 0.0)
+            tap = jnp.where(
+                ahead_of == first + o, jnp.concatenate([same] * (MW // 128), axis=1), 0.0
+            )
             r.ms[b, i * MB : (i + 1) * MB] = tap.astype(BF16)
+
+    loop(T // MB, shift_matrices)
 
     lane = lax.broadcasted_iota(jnp.int32, (1, 128), 1)
     lane_f = lane.astype(F32)
@@ -1494,11 +1495,13 @@
         return jnp.where(at == q % repeats, tiled, jnp.zeros_like(tiled))
 
     segs = placed(segment_ids, plan.sr)
-    segs = jnp.broadcast_to(segs[:, None, :], (seqs, 8, plan.sw))
     norms = placed(jnp.concatenate([norm_gain, norm_bias], 0), plan.nr)
-    norms = norms.reshape(plan.srows, plan.FFn)
-    small = jnp.concatenate([norms, mid_gain[None], mid_bias[None], depth_weight], 0)
-    small = jnp.pad(small, ((0, plan.spack - small.shape[0]), (0, 0)))
+    rows = plan.spack
+    at = lax.broadcasted_iota(jnp.int32, (rows, plan.FFn), 0)
+    small = jnp.pad(norms, ((0, rows - 8), (0, plan.FFn - plan.nw)))
+    small = jnp.where(at == 8, mid_gain[None], jnp.where(at == 9, mid_bias[None], small))
+    taps = jnp.pad(depth_weight, ((10, rows - 10 - depth_weight.shape[0]), (0, 0)))
+    small = jnp.where(at >= 10, taps, small)
     weights = [None] * WEIGHTS
     weights[GLU], weights[CONV], weights[LEFT] = glu_weight, conv_weight, left_weight
     weights[POINT], weights[QKV], weights[OUT] = point_weight, qkv_weight, out_weight

time: 159 us -> 157 us (0.987)
    concatenate x2 -> x0, other arithmetic: 2.06 us -> none  [the longest x1 1.36 us: local(): jnp.concatenate([norms, mid_gain[None], mid_bias[None], depth_weight], 0)]
where the time goes in v2:
time: 157 us
  Pallas kernels  154 us (98%)
    pallas_call x1, Pallas kernels, local(): pl.pallas_call(lambda *refs: kernel(plan, *refs), out_shape=out_shape, in...  148 us
    pallas_call x1, Pallas kernels, unpacked(): pl.pallas_call(body, out_shape=out_shape, in_specs=[hbm] * count + [vmem]...  6.07 us

profile of v2, /device:TPU:0, one launch (start us, length us, event | category | flops | bytes accessed | tf_op | source)
XLA Modules:
  0.0 157.2 jit_solution(8836805143809744339)
XLA Ops:
  0.7 0.0 copy-start.3
  0.7 0.0 copy-start.1
  0.7 0.0 copy-start.2
  0.7 0.0 copy-start
  0.7 0.6 copy-done.3
  1.3 0.0 copy-done.1
  1.4 0.0 copy-done.2
  1.4 0.0 copy-done
  1.4 1.4 fusion.8.refs_3_
  2.8 148.1 %cell.1 = (bf16[2,256,512]{2,1,0:T(8,128)(2,1)}, bf16[2,256,512]{2,1,0:T(8,128)(2,1)}, bf16[128,1024]{1,0:T(8,128)(2,1)}, bf16[128,768]{1,0:T(8,128)(2,1)}, bf16...) custom-call(bf16[2,256,512]{2,1,0:T(8,128)(2,1)} %refs_0_.1, ...), custom_call_target="tpu_custom_call" | custom-call | tf_op jit(solution)/shard_map/cell/pallas_call | solution.py:1516
  150.9 6.1 %shard_map.271 = (f32[2,256,512]{2,1,0:T(8,128)}, f32[2,256,512]{2,1,0:T(8,128)}, f32[128,1024]{1,0:T(8,128)}, f32[3,128,256]{2,1,0:T(8,128)}, f32[128,2048]{1,0...) custom-call(bf16[2,256,512]{2,1,0:T(8,128)(2,1)} %get-tuple-element., ...), custom_call_target="tpu_custom_call" | custom-call | tf_op jit(solution)/shard_map/pallas_call | solution.py:1598
  (2 shorter events, 0.0 us)
Async XLA Ops:
  0.7 0.7 copy-start.3
  0.7 0.7 copy-start.1
  0.7 0.7 copy-start.2
  0.7 0.7 copy-start

commit v3 on v2

--- a/solution.py
+++ b/solution.py
@@ -20,39 +20,39 @@
 UNIT_WEIGHT = (GLU, GLU, CONV, LEFT, LEFT, POINT, POINT, QKV, QKV, OUT, FIN, FOUT, WEIGHTS)
 UNIT_PART = (0, 1, None, 0, 1, 0, 1, 0, 1, None, None, None, None)
 
-SHARED = (GLU, CONV, POINT,)
+SHARED = (GLU, LEFT, POINT, FIN,)
 SMALLS, TOKENS = 8, 9
-START = (GLU, CONV, SMALLS, TOKENS)
+START = (GLU, SMALLS, CONV, LEFT, TOKENS)
 FORWARD = (
-    ((1, GLU), (1, CONV)),
-    (),
-    ((0, LEFT),),
-    ((2, GLU), (2, CONV), (0, POINT), (3, GLU)),
-    ((1, LEFT),),
-    ((1, POINT), (3, CONV)),
-    ((0, QKV),),
-    (),
-    (),
-    (),
-    ((2, LEFT),),
-    ((2, POINT), (0, OUT), (0, FIN)),
+    ((1, GLU),),
+    (),
+    ((1, CONV),),
+    ((1, LEFT), (2, GLU), (0, POINT), (2, CONV), (2, LEFT), (0, QKV), (3, GLU), (1, POINT)),
+    (),
+    ((0, OUT),),
+    ((0, FIN),),
+    (),
     (),
     ((1, QKV),),
     (),
-    ((1, OUT),),
-    (),
-    (),
-    ((3, POINT), (0, FOUT)),
+    ((3, LEFT), (2, POINT), (1, OUT)),
+    (),
     ((1, FIN),),
-    (),
-    (),
-    (),
-    ((2, QKV), (2, OUT)),
+    ((0, FOUT),),
+    ((2, QKV),),
+    (),
+    ((2, OUT),),
+    ((3, POINT), (2, FIN)),
+    ((0, TOKENS),),
+    (),
+    (),
     (),
     (),
     ((1, FOUT),),
-    ((0, TOKENS),),
-    ((2, FIN),),
+    (),
+    (),
+    ((3, FIN),),
+    (),
     ((2, FOUT),),
     (),
     (),
@@ -232,6 +232,7 @@
         r.y1 = vm((T, D), F32)
         r.a2 = vm((T, D), BF16)
         r.pext = vm((3, T + 16, H), F32)
+        r.rgl = vm((T, H), F32)
         r.dgl = vm((T, FF), BF16)
         r.dgr = vm((T, H), BF16)
         r.nm = vm((T, FF), BF16)
@@ -986,18 +987,12 @@
     g3(CONV)
 
     def conv(i):
+        i = c * i + oc * (NB - 1 - i)
         a2 = r.a2[rows_of(i)]
         for o in range(3):
             r.pext[o, rows_of(i, RB, 8)] = mm(a2, r.w[CONV][o])
 
-    loop(NB, conv)
-    edge_send(0, r.pext[0, T : T + 8], r.pext[2, 8:16])
-    pass_turn()
-    top, bottom = edge_take(0)
-    r.pext[0, 0:8] = top
-    r.pext[2, T + 8 : T + 16] = bottom
-    pass_turn()
-    for k in range(T // 128):
+    def right(k):
         lo = k * 128
         before = mask(-1, lo, 128)
         after = mask(1, lo, 128)
@@ -1007,8 +1002,21 @@
             + r.pext[2, lo + 9 : lo + 137] * jnp.concatenate([after] * (H // 128), axis=1)
         )
         value, slope = gelu_both(pre)
-        r.pext[1, lo + 8 : lo + 136] = value
+        r.rgl[lo : lo + 128] = value
         r.dgr[lo : lo + 128] = slope.astype(BF16)
+
+    edge = (0, lambda: edge_send(0, r.pext[0, T : T + 8], r.pext[2, 8:16]))
+    loop(NB, conv, [edge])
+    pass_turn()
+    blocks = range(T // 128)
+    for k in blocks[1:-1]:
+        right(k)
+    pass_turn()
+    top, bottom = edge_take(0)
+    r.pext[0, 0:8] = top
+    r.pext[2, T + 8 : T + 16] = bottom
+    right(blocks[0])
+    right(blocks[-1])
     pass_turn()
     pass_turn()
     g3(LEFT)
@@ -1016,21 +1024,25 @@
     CH = 512
     RM = 128
 
+    def inner_first(i, count):
+        return c * i + oc * (count - 1 - i)
+
     def left(i):
+        i = inner_first(i, T // RM)
         rows, erows = rows_of(i, RM), rows_of(i, RM, 8)
         a2 = r.a2[rows]
         for k in range(FF // CH):
             value, slope = gelu_both(mm(a2, r.w[LEFT][:, k * CH : (k + 1) * CH]))
             r.dgl[rows, k * CH : (k + 1) * CH] = slope.astype(BF16)
             r.big[erows, k * CH : (k + 1) * CH] = value
-        r.big[erows, 0:H] += r.pext[1, erows]
+        r.big[erows, 0:H] += r.rgl[rows]
         unit, rs = normed(r.big[erows])
         r.nm[rows] = unit.astype(BF16)
         r.rm[rows] = rs
         r.hid[rows_of(i, RM, 16)] = (unit * r.midp[0:1] + r.midp[1:2]).astype(BF16)
 
-    loop(T // RM, left, pass_turns(T // RM))
-    edge_send(1, r.hid[T : T + 16], r.hid[16:32])
+    edge = (0, lambda: edge_send(1, r.hid[T : T + 16], r.hid[16:32]))
+    loop(T // RM, left, [edge] + pass_turns(T // RM))
     r.hid[0:16], r.hid[T + 16 : T + 32] = edge_take(1)
     pass_turn()
 

time: 157 us -> 155 us (0.987)
  Pallas kernels: 154 us -> 152 us
    pallas_call x1, Pallas kernels: 148 us -> 146 us  [local(): pl.pallas_call(lambda *refs: kernel(plan, *refs), out_shape=out_shape, in...]
where the time goes in v3:
time: 155 us
  Pallas kernels  152 us (98%)
    pallas_call x1, Pallas kernels, local(): pl.pallas_call(lambda *refs: kernel(plan, *refs), out_shape=out_shape, in...  146 us
    pallas_call x1, Pallas kernels, unpacked(): pl.pallas_call(body, out_shape=out_shape, in_specs=[hbm] * count + [vmem]...  6.07 us

profile of v3, /device:TPU:0, one launch (start us, length us, event | category | flops | bytes accessed | tf_op | source)
XLA Modules:
  0.0 155.1 jit_solution(4272398240412503934)
XLA Ops:
  0.7 0.0 copy-start.3
  0.7 0.0 copy-start.1
  0.7 0.0 copy-start.2
  0.7 0.0 copy-start
  0.7 0.6 copy-done.3
  1.3 0.0 copy-done.1
  1.4 0.0 copy-done.2
  1.4 0.0 copy-done
  1.4 1.4 fusion.8.refs_3_
  2.8 146.0 %cell.1 = (bf16[2,256,512]{2,1,0:T(8,128)(2,1)}, bf16[2,256,512]{2,1,0:T(8,128)(2,1)}, bf16[128,1024]{1,0:T(8,128)(2,1)}, bf16[128,768]{1,0:T(8,128)(2,1)}, bf16...) custom-call(bf16[2,256,512]{2,1,0:T(8,128)(2,1)} %refs_0_.1, ...), custom_call_target="tpu_custom_call" | custom-call | tf_op jit(solution)/shard_map/cell/pallas_call | solution.py:1528
  148.8 6.1 %shard_map.271 = (f32[2,256,512]{2,1,0:T(8,128)}, f32[2,256,512]{2,1,0:T(8,128)}, f32[128,1024]{1,0:T(8,128)}, f32[3,128,256]{2,1,0:T(8,128)}, f32[128,2048]{1,0...) custom-call(bf16[2,256,512]{2,1,0:T(8,128)(2,1)} %get-tuple-element., ...), custom_call_target="tpu_custom_call" | custom-call | tf_op jit(solution)/shard_map/pallas_call | solution.py:1610
  (2 shorter events, 0.0 us)
Async XLA Ops:
  0.7 0.7 copy-start.3
  0.7 0.7 copy-start.1
  0.7 0.7 copy-start.2
  0.7 0.7 copy-start

commit v4 on v3

--- a/solution.py
+++ b/solution.py
@@ -133,7 +133,7 @@
     t = jnp.tanh(v * (c + (c * 0.044715) * sq))
     half = 0.5 * t + 0.5
     value = v * half
-    slope = half + (0.5 * v) * (1.0 - t * t) * (c + (3.0 * c * 0.044715) * sq)
+    slope = half + (value * (1.0 - half)) * (2.0 * c + (6.0 * c * 0.044715) * sq)
     return value, slope
 
 

time: 155 us -> 155 us (level)
  no operation moved by 1% of the time
where the time goes in v4:
time: 155 us
  Pallas kernels  152 us (98%)
    pallas_call x1, Pallas kernels, local(): pl.pallas_call(lambda *refs: kernel(plan, *refs), out_shape=out_shape, in...  146 us
    pallas_call x1, Pallas kernels, unpacked(): pl.pallas_call(body, out_shape=out_shape, in_specs=[hbm] * count + [vmem]...  6.07 us

profile of v4, /device:TPU:0, one launch (start us, length us, event | category | flops | bytes accessed | tf_op | source)
XLA Modules:
  0.0 154.7 jit_solution(10712299610364608142)
XLA Ops:
  0.7 0.0 copy-start.3
  0.7 0.0 copy-start.1
  0.7 0.0 copy-start.2
  0.7 0.0 copy-start
  0.7 0.6 copy-done.3
  1.3 0.0 copy-done.1
  1.4 0.0 copy-done.2
  1.4 0.0 copy-done
  1.4 1.4 fusion.8.refs_3_
  2.8 145.7 %cell.1 = (bf16[2,256,512]{2,1,0:T(8,128)(2,1)}, bf16[2,256,512]{2,1,0:T(8,128)(2,1)}, bf16[128,1024]{1,0:T(8,128)(2,1)}, bf16[128,768]{1,0:T(8,128)(2,1)}, bf16...) custom-call(bf16[2,256,512]{2,1,0:T(8,128)(2,1)} %refs_0_.1, ...), custom_call_target="tpu_custom_call" | custom-call | tf_op jit(solution)/shard_map/cell/pallas_call | solution.py:1528
  148.5 6.1 %shard_map.271 = (f32[2,256,512]{2,1,0:T(8,128)}, f32[2,256,512]{2,1,0:T(8,128)}, f32[128,1024]{1,0:T(8,128)}, f32[3,128,256]{2,1,0:T(8,128)}, f32[128,2048]{1,0...) custom-call(bf16[2,256,512]{2,1,0:T(8,128)(2,1)} %get-tuple-element., ...), custom_call_target="tpu_custom_call" | custom-call | tf_op jit(solution)/shard_map/pallas_call | solution.py:1610
  (2 shorter events, 0.0 us)
Async XLA Ops:
  0.7 0.7 copy-start.3
  0.7 0.7 copy-start.1
  0.7 0.7 copy-start.2
  0.7 0.7 copy-start
